TPU v7x, 256 devices: a whole 4x4x8 slice. The times are simulated.
256 devices in a mesh: stream: 16 (over z, core), cross: 16 (over x, y).
Axes of the slice: x: 4, y: 4, z: 8, core: 2. Of those that a mesh axis runs over, the one named last changes fastest.
Arguments:
- rhs: float32 [1024, 4096], P('stream', 'cross'), may hold values from -6 to 6
- previous: float32 [1024, 4096], P('stream', 'cross'), may hold values from -6 to 6
- dinv: bfloat16 [1024, 64, 4096], P('stream', 'cross'), may hold values from -1 to 2, as said below
- lower: bfloat16 [1024, 64, 4096], P('stream', 'cross'), may hold values from -0.3125 to 0.3125
- spike: bfloat16 [1024, 64, 4096], P('stream', 'cross'), may hold values from -1 to 1.5
- coupling: bfloat16 [1024, 64, 2, 4096], P('stream', 'cross'), may hold values from -0.5 to 0.5
- nbr_line: int32 [1024, 64, 2], P('stream', 'cross'), may hold values from 0 to 63, as said below
- nbr_shift: int32 [1024, 64, 2], P('stream', 'cross'), may hold values from 0 to 2
Outputs:
- sweep: float32 [1024, 4096], P('stream', 'cross')
Inputs may be any that keep to these rules, and one draw needn't show every extreme that they name: `dinv`: diagonal entries lie between 0.3 and 1.4, the others are small. `nbr_line`: the lines form a cross-section of rows of 4 lines; every element of line l reaches line l - 4 across one face and line l + 4 across the other, except on the first and last row, where both faces reach the one neighbouring row; which face is which is fixed along each line.
All inputs are finite; a program needn't handle non-finite values.
Results may differ from a plain program's by a relative error of at most 0.0004.
Values sent between devices are 32-bit elements; how exact they have to be, the bound alone decides.
No kernel may reach another device: no remote copies, remote signals or barrier semaphores. Data moves between devices by JAX's collectives and lax.ppermute only.
A program may use at most 128 MiB of HBM per device.

v0:
```python
import jax
import jax.numpy as jnp
from jax import lax
from jax.sharding import PartitionSpec as P

UNKNOWNS = 64
SPAN = 16


precise = lax.Precision.HIGHEST


def padded_2(block, sides, width):
    for axis, dim in sides:
        count = lax.axis_size(axis)
        forward = [(i, i + 1) for i in range(count - 1)]
        backward = [(target, source) for source, target in forward]
        low = lax.ppermute(
            lax.slice_in_dim(block, block.shape[dim] - width, None, axis=dim), axis, forward
        )
        high = lax.ppermute(lax.slice_in_dim(block, 0, width, axis=dim), axis, backward)
        block = jnp.concatenate([low, block, high], axis=dim)
    return block


def shifted(shard, axis, by):
    length = lax.axis_size(axis)
    pairs = [(i, i + by) for i in range(length) if 0 <= i + by < length]
    return lax.ppermute(shard, axis, pairs)


def on_device(rhs, previous, dinv, lower, spike, coupling, nbr_line, nbr_shift):
    block_width = UNKNOWNS
    elements = rhs.shape[0]
    lines_dev = rhs.shape[1] // block_width
    line_groups = elements // SPAN
    padded = padded_2(previous, (("stream", 0),), 1)
    row_index = lax.broadcasted_iota(jnp.int32, nbr_shift.shape, 0) + nbr_shift
    bordered = padded_2(padded, (("cross", 1),), lines_dev * block_width)
    lookup = bordered.reshape(elements + 2, 3 * lines_dev, block_width)
    first_line = lax.axis_index("cross") * lines_dev - lines_dev
    relative = jnp.clip(nbr_line - first_line, 0, 3 * lines_dev - 1)
    picked = lookup[row_index, relative]
    couple_mat = coupling.reshape(elements, lines_dev, coupling.shape[2], block_width, block_width)
    coupled = jnp.einsum(
        "elfij,elfj->eli", couple_mat, picked, precision=precise, preferred_element_type=jnp.float32
    )
    residual = (rhs.reshape(elements, lines_dev, block_width) - coupled).reshape(
        line_groups, SPAN, lines_dev, block_width
    )
    inverse_mat = dinv.reshape(line_groups, SPAN, lines_dev, block_width, block_width)
    lower_mat = lower.reshape(line_groups, SPAN, lines_dev, block_width, block_width)
    spike_mat = spike.reshape(line_groups, SPAN, lines_dev, block_width, block_width)

    def advance(position, status):
        earlier, local_sol = status
        inverse_now = lax.dynamic_index_in_dim(inverse_mat, position, 1, keepdims=False)
        lower_now = lax.dynamic_index_in_dim(lower_mat, position, 1, keepdims=False)
        residual_now = lax.dynamic_index_in_dim(residual, position, 1, keepdims=False)
        balance = residual_now - jnp.einsum(
            "blij,blj->bli",
            lower_now,
            earlier,
            precision=precise,
            preferred_element_type=jnp.float32,
        )
        following = jnp.einsum(
            "blij,blj->bli",
            inverse_now,
            balance,
            precision=precise,
            preferred_element_type=jnp.float32,
        )
        local_sol = lax.dynamic_update_index_in_dim(local_sol, following, position, 1)
        return (following, local_sol)

    zero_vec = jnp.zeros((line_groups, lines_dev, block_width), jnp.float32)
    zero_sol = jnp.zeros((line_groups, SPAN, lines_dev, block_width), jnp.float32)
    _, local_sol = lax.fori_loop(0, SPAN, advance, (zero_vec, zero_sol))
    spike_last = spike_mat[:, SPAN - 1]
    local_last = local_sol[:, SPAN - 1]

    def compose(block_no, status):
        transfer_mat, offset_vec = status
        spike_now = lax.dynamic_index_in_dim(spike_last, block_no, 0, keepdims=False)
        local_now = lax.dynamic_index_in_dim(local_last, block_no, 0, keepdims=False)
        transfer_mat = jnp.einsum(
            "lij,ljk->lik",
            spike_now,
            transfer_mat,
            precision=precise,
            preferred_element_type=jnp.float32,
        )
        offset_vec = (
            jnp.einsum(
                "lij,lj->li",
                spike_now,
                offset_vec,
                precision=precise,
                preferred_element_type=jnp.float32,
            )
            + local_now
        )
        return (transfer_mat, offset_vec)

    identity_mat = jnp.broadcast_to(
        jnp.eye(block_width, dtype=jnp.float32), (lines_dev, block_width, block_width)
    )
    zero_flow = jnp.zeros((lines_dev, block_width), jnp.float32)
    device_map, offset = lax.fori_loop(0, line_groups, compose, (identity_mat, zero_flow))

    def relay(relay_turn, inflow):
        outflow = offset + jnp.einsum("lij,lj->li", device_map, inflow, precision=precise)
        return shifted(outflow, "stream", 1)

    inflow = lax.fori_loop(0, lax.axis_size("stream") - 1, relay, zero_flow)

    def spread(block_no, status):
        current, stored = status
        stored = lax.dynamic_update_index_in_dim(stored, current, block_no, 0)
        spike_now = lax.dynamic_index_in_dim(spike_last, block_no, 0, keepdims=False)
        local_now = lax.dynamic_index_in_dim(local_last, block_no, 0, keepdims=False)
        current = local_now + jnp.einsum(
            "lij,lj->li", spike_now, current, precision=precise, preferred_element_type=jnp.float32
        )
        return (current, stored)

    _, inflows = lax.fori_loop(0, line_groups, spread, (inflow, zero_vec))
    swept = local_sol + jnp.einsum(
        "bklij,blj->bkli", spike_mat, inflows, precision=precise, preferred_element_type=jnp.float32
    )
    return swept.reshape(elements, lines_dev * block_width)


def solution(mesh):
    return jax.shard_map(
        on_device,
        mesh=mesh,
        in_specs=(
            P("stream", "cross"),
            P("stream", "cross"),
            P("stream", "cross", None),
            P("stream", "cross", None),
            P("stream", "cross", None),
            P("stream", "cross", None, None),
            P("stream", "cross", None),
            P("stream", "cross", None),
        ),
        out_specs=P("stream", "cross"),
        check_vma=False,
    )
```

profile of v0, /device:TPU:154, one launch (start us, length us, event | category | flops | bytes accessed | tf_op | source)
XLA Modules:
  0.0 227.3 jit_solution(4088791415258234697)
XLA Ops:
  2.6 4.9 %collective-permute-start.2 = (f32[1,256]{1,0:T(1,128)S(1)}, f32[1,256]{1,0:T(1,128)S(1)}, u32[]{:S(2)}, u32[]{:S(2)}) collective-permute-start(f32[1,256]{1,0:T(1,128)S(1)} %get-tuple-element.399), channel_id=1, source_target_pairs={{16,0},{32,16},{48,32},{64,48},{80,64},{96,80},{112,96},{128,112},... | collective-permute-start | bytes 3080 | tf_op jit(solution)/shard_map/ppermute | solution.py:21
  10.3 5.6 %reshape.30 = bf16[4,16,4,64,64]{4,3,1,0,2:T(8,128)(2,1)} reshape(bf16[64,4,4096]{2,0,1:T(8,128)(2,1)S(1)} %copy.12) | data formatting | bytes 4194304 | tf_op jit(solution)/shard_map/reshape | solution.py:53
  17.2 14.4 %reshape.27 = bf16[64,4,2,64,64]{4,3,2,1,0:T(8,128)(2,1)} reshape(bf16[64,4,2,4096]{3,2,1,0:T(2,128)(2,1)} %param.21) | data formatting | bytes 8388608 | tf_op jit(solution)/shard_map/reshape | solution.py:44
  31.7 4.5 %reshape.24 = bf16[4,16,4,64,64]{4,3,2,1,0:T(8,128)(2,1)} reshape(bf16[64,4,4096]{2,1,0:T(4,128)(2,1)S(1)} %copy-done) | data formatting | bytes 4194304 | tf_op jit(solution)/shard_map/reshape | solution.py:51
  36.2 7.0 %reshape.29 = bf16[4,16,4,64,64]{4,3,2,1,0:T(8,128)(2,1)} reshape(bf16[64,4,4096]{2,1,0:T(4,128)(2,1)} %param.19) | data formatting | bytes 4194304 | tf_op jit(solution)/shard_map/reshape | solution.py:52
  49.5 5.2 %collective-permute-done.4 = f32[66,256]{1,0:T(8,128)S(1)} collective-permute-done((f32[66,256]{1,0:T(8,128)S(1)}, f32[66,256]{1,0:T(8,128)S(1)}, u32[]{:S(2)}, u32[]{:S(2)}) %collective-permute-start.4) | collective-permute-done | bytes 67616 | tf_op jit(solution)/shard_map/ppermute | solution.py:21
  58.5 8.9 %fusion.30 = f32[64,4,1,64,1]{3,2,4,1,0:T(1,128)S(1)} fusion(f32[64,4,2,64,1]{3,4,2,1,0:T(1,128)S(1)} %bitcast.141, bf16[64,4,2,64,64]{4,3,2,1,0:T(8,128)(2,1)} %reshape.27), kind=kOutput, calls=%fused_computation.45 | convolution fusion | flops 25165824 | bytes 4390912 | tf_op jit(solution)/shard_map/elfij,elfj->eli/dot_general | solution.py:45
  67.5 47.4 %while.56 = (s32[]{:T(128)}, f32[4,4,64]{2,1,0:T(4,128)S(1)}, f32[4,16,4,64]{3,2,1,0:T(4,128)S(1)}, bf16[4,16,4,64,64]{4,3,2,1,0:T(8,128)(2,1)}, f32[4,16,4,64]{...) while((s32[]{:T(128)}, f32[4,4,64]{2,1,0:T(4,128)S(1)}, f32[4,16,4,64]{3,2,1,0:T(4,128)S(1)}, ...), condition=%wide.region_1.2_spmd, body=%wide.region_0.1_spmd.sunk | while | flops 1573890 | bytes 570453 | solution.py:79
  116.9 96.6 %while.57 = (s32[]{:T(128)}, f32[4,64]{1,0:T(4,128)S(1)}, f32[4,64,64]{2,1,0:T(8,128)S(1)}, f32[4,64]{1,0:T(4,128)S(1)}, s32[]{:T(128)}) while((s32[]{:T(128)}, f32[4,64]{1,0:T(4,128)S(1)}, f32[4,64,64]{2,1,0:T(8,128)S(1)}, f32[4,64]{1,0:T(4,128)S(1)}, s32[]{:T(128)}) %tuple.100), condition=%wide.region_5.6_spmd, body=%wide.region_4.5_spmd.sunk | while | flops 196866 | bytes 74853 | solution.py:116
  119.2 4.2 %collective-permute-done = f32[4,64]{1,0:T(4,128)S(1)} collective-permute-done((f32[4,64]{1,0:T(4,128)S(1)}, f32[4,64]{1,0:T(4,128)S(1)}, u32[]{:S(2)}, u32[]{:S(2)}) %collective-permute-start) | collective-permute-done | bytes 1056 | tf_op jit(solution)/shard_map/while/body/eval_jaxpr/ppermute | solution.py:29
  125.6 4.2 %collective-permute-done = f32[4,64]{1,0:T(4,128)S(1)} collective-permute-done((f32[4,64]{1,0:T(4,128)S(1)}, f32[4,64]{1,0:T(4,128)S(1)}, u32[]{:S(2)}, u32[]{:S(2)}) %collective-permute-start) | collective-permute-done | bytes 1056 | tf_op jit(solution)/shard_map/while/body/eval_jaxpr/ppermute | solution.py:29
  132.0 4.2 %collective-permute-done = f32[4,64]{1,0:T(4,128)S(1)} collective-permute-done((f32[4,64]{1,0:T(4,128)S(1)}, f32[4,64]{1,0:T(4,128)S(1)}, u32[]{:S(2)}, u32[]{:S(2)}) %collective-permute-start) | collective-permute-done | bytes 1056 | tf_op jit(solution)/shard_map/while/body/eval_jaxpr/ppermute | solution.py:29
  138.5 4.2 %collective-permute-done = f32[4,64]{1,0:T(4,128)S(1)} collective-permute-done((f32[4,64]{1,0:T(4,128)S(1)}, f32[4,64]{1,0:T(4,128)S(1)}, u32[]{:S(2)}, u32[]{:S(2)}) %collective-permute-start) | collective-permute-done | bytes 1056 | tf_op jit(solution)/shard_map/while/body/eval_jaxpr/ppermute | solution.py:29
  144.9 4.2 %collective-permute-done = f32[4,64]{1,0:T(4,128)S(1)} collective-permute-done((f32[4,64]{1,0:T(4,128)S(1)}, f32[4,64]{1,0:T(4,128)S(1)}, u32[]{:S(2)}, u32[]{:S(2)}) %collective-permute-start) | collective-permute-done | bytes 1056 | tf_op jit(solution)/shard_map/while/body/eval_jaxpr/ppermute | solution.py:29
  151.3 4.2 %collective-permute-done = f32[4,64]{1,0:T(4,128)S(1)} collective-permute-done((f32[4,64]{1,0:T(4,128)S(1)}, f32[4,64]{1,0:T(4,128)S(1)}, u32[]{:S(2)}, u32[]{:S(2)}) %collective-permute-start) | collective-permute-done | bytes 1056 | tf_op jit(solution)/shard_map/while/body/eval_jaxpr/ppermute | solution.py:29
  157.8 4.2 %collective-permute-done = f32[4,64]{1,0:T(4,128)S(1)} collective-permute-done((f32[4,64]{1,0:T(4,128)S(1)}, f32[4,64]{1,0:T(4,128)S(1)}, u32[]{:S(2)}, u32[]{:S(2)}) %collective-permute-start) | collective-permute-done | bytes 1056 | tf_op jit(solution)/shard_map/while/body/eval_jaxpr/ppermute | solution.py:29
  164.2 4.2 %collective-permute-done = f32[4,64]{1,0:T(4,128)S(1)} collective-permute-done((f32[4,64]{1,0:T(4,128)S(1)}, f32[4,64]{1,0:T(4,128)S(1)}, u32[]{:S(2)}, u32[]{:S(2)}) %collective-permute-start) | collective-permute-done | bytes 1056 | tf_op jit(solution)/shard_map/while/body/eval_jaxpr/ppermute | solution.py:29
  170.7 4.2 %collective-permute-done = f32[4,64]{1,0:T(4,128)S(1)} collective-permute-done((f32[4,64]{1,0:T(4,128)S(1)}, f32[4,64]{1,0:T(4,128)S(1)}, u32[]{:S(2)}, u32[]{:S(2)}) %collective-permute-start) | collective-permute-done | bytes 1056 | tf_op jit(solution)/shard_map/while/body/eval_jaxpr/ppermute | solution.py:29
  177.1 4.2 %collective-permute-done = f32[4,64]{1,0:T(4,128)S(1)} collective-permute-done((f32[4,64]{1,0:T(4,128)S(1)}, f32[4,64]{1,0:T(4,128)S(1)}, u32[]{:S(2)}, u32[]{:S(2)}) %collective-permute-start) | collective-permute-done | bytes 1056 | tf_op jit(solution)/shard_map/while/body/eval_jaxpr/ppermute | solution.py:29
  183.5 4.2 %collective-permute-done = f32[4,64]{1,0:T(4,128)S(1)} collective-permute-done((f32[4,64]{1,0:T(4,128)S(1)}, f32[4,64]{1,0:T(4,128)S(1)}, u32[]{:S(2)}, u32[]{:S(2)}) %collective-permute-start) | collective-permute-done | bytes 1056 | tf_op jit(solution)/shard_map/while/body/eval_jaxpr/ppermute | solution.py:29
  190.0 4.2 %collective-permute-done = f32[4,64]{1,0:T(4,128)S(1)} collective-permute-done((f32[4,64]{1,0:T(4,128)S(1)}, f32[4,64]{1,0:T(4,128)S(1)}, u32[]{:S(2)}, u32[]{:S(2)}) %collective-permute-start) | collective-permute-done | bytes 1056 | tf_op jit(solution)/shard_map/while/body/eval_jaxpr/ppermute | solution.py:29
  196.4 4.2 %collective-permute-done = f32[4,64]{1,0:T(4,128)S(1)} collective-permute-done((f32[4,64]{1,0:T(4,128)S(1)}, f32[4,64]{1,0:T(4,128)S(1)}, u32[]{:S(2)}, u32[]{:S(2)}) %collective-permute-start) | collective-permute-done | bytes 1056 | tf_op jit(solution)/shard_map/while/body/eval_jaxpr/ppermute | solution.py:29
  202.8 4.2 %collective-permute-done = f32[4,64]{1,0:T(4,128)S(1)} collective-permute-done((f32[4,64]{1,0:T(4,128)S(1)}, f32[4,64]{1,0:T(4,128)S(1)}, u32[]{:S(2)}, u32[]{:S(2)}) %collective-permute-start) | collective-permute-done | bytes 1056 | tf_op jit(solution)/shard_map/while/body/eval_jaxpr/ppermute | solution.py:29
  214.4 12.0 %fusion.20 = f32[4,4,1,16,64]{4,2,3,1,0:T(1,128)S(1)} fusion(f32[4,4,64,1,1]{2,3,4,1,0:T(1,128)S(1)} %bitcast.148, bf16[4,16,4,64,64]{4,3,1,0,2:T(8,128)(2,1)} %reshape.30), kind=kOutput, calls=%fused_computation.27 | convolution fusion | flops 12582912 | bytes 2166784 | tf_op jit(solution)/shard_map/bklij,blj->bkli/dot_general | solution.py:129
  (184 shorter events, 108.5 us)
Async XLA Ops:
  0.7 42.5 %collective-permute-start.1 = (f32[1,256]{1,0:T(1,128)S(1)}, f32[1,256]{1,0:T(1,128)S(1)}, u32[]{:S(2)}, u32[]{:S(2)}) collective-permute-start(f32[1,256]{1,0:T(1,128)S(1)} %get-tuple-element.398), channel_id=1, source_target_pairs={{0,16},{16,32},{32,48},{48,64},{64,80},{80,96},{96,112},{112,128},... | collective-permute-start | bytes 3080 | tf_op jit(solution)/shard_map/ppermute | solution.py:18
  2.6 40.6 %collective-permute-start.2 = (f32[1,256]{1,0:T(1,128)S(1)}, f32[1,256]{1,0:T(1,128)S(1)}, u32[]{:S(2)}, u32[]{:S(2)}) collective-permute-start(f32[1,256]{1,0:T(1,128)S(1)} %get-tuple-element.399), channel_id=1, source_target_pairs={{16,0},{32,16},{48,32},{64,48},{80,64},{96,80},{112,96},{128,112},... | collective-permute-start | bytes 3080 | tf_op jit(solution)/shard_map/ppermute | solution.py:21
  10.2 6.6 %copy-start.3 = (s32[64,4,2]{0,2,1:T(2,128)S(1)}, s32[64,4,2]{0,2,1:T(2,128)}, u32[]{:S(2)}) copy-start(s32[64,4,2]{0,2,1:T(2,128)} %param.22) | copy-start | bytes 6148
  10.3 6.6 %copy-start.4 = (s32[64,4,2]{0,2,1:T(2,128)S(1)}, s32[64,4,2]{0,2,1:T(2,128)}, u32[]{:S(2)}) copy-start(s32[64,4,2]{0,2,1:T(2,128)} %param.23) | copy-start | bytes 6148
  17.2 14.4 %copy-start.2 = (f32[64,256]{1,0:T(8,128)S(1)}, f32[64,256]{1,0:T(8,128)}, u32[]{:S(2)}) copy-start(f32[64,256]{1,0:T(8,128)} %param.16) | copy-start | bytes 196612
  17.2 14.5 %copy-start = (bf16[64,4,4096]{2,1,0:T(4,128)(2,1)S(1)}, bf16[64,4,4096]{2,1,0:T(4,128)(2,1)}, u32[]{:S(2)}) copy-start(bf16[64,4,4096]{2,1,0:T(4,128)(2,1)} %param.18) | copy-start | bytes 6291460
  36.2 7.1 %copy-start.1 = (f32[64,256]{1,0:T(8,128)S(1)}, f32[64,256]{1,0:T(8,128)}, u32[]{:S(2)}) copy-start(f32[64,256]{1,0:T(8,128)} %param.17) | copy-start | bytes 196612
  43.3 6.2 %collective-permute-start.3 = (f32[66,256]{1,0:T(8,128)S(1)}, f32[66,256]{1,0:T(8,128)S(1)}, u32[]{:S(2)}, u32[]{:S(2)}) collective-permute-start(f32[66,256]{1,0:T(8,128)S(1)} %pad_maximum_fusion.1), channel_id=1, source_target_pairs={{0,1},{1,2},{2,3},{3,4},{4,5},{5,6},{6,7},{7,8},{8,9},{9,10},{10,1... | collective-permute-start | bytes 202760 | tf_op jit(solution)/shard_map/ppermute | solution.py:18
  46.4 8.4 %collective-permute-start.4 = (f32[66,256]{1,0:T(8,128)S(1)}, f32[66,256]{1,0:T(8,128)S(1)}, u32[]{:S(2)}, u32[]{:S(2)}) collective-permute-start(f32[66,256]{1,0:T(8,128)S(1)} %pad_maximum_fusion.1), channel_id=1, source_target_pairs={{1,0},{2,1},{3,2},{4,3},{5,4},{6,5},{7,6},{8,7},{9,8},{10,9},{11,1... | collective-permute-start | bytes 202760 | tf_op jit(solution)/shard_map/ppermute | solution.py:21
  117.2 6.1 %collective-permute-start = (f32[4,64]{1,0:T(4,128)S(1)}, f32[4,64]{1,0:T(4,128)S(1)}, u32[]{:S(2)}, u32[]{:S(2)}) collective-permute-start(f32[4,64]{1,0:T(4,128)S(1)} %add.151), channel_id=1, source_target_pairs={{0,16},{16,32},{32,48},{48,64},{64,80},{80,96},{96,112},{112,128},... | collective-permute-start | bytes 3080 | tf_op jit(solution)/shard_map/while/body/eval_jaxpr/ppermute | solution.py:29
  123.7 6.1 %collective-permute-start = (f32[4,64]{1,0:T(4,128)S(1)}, f32[4,64]{1,0:T(4,128)S(1)}, u32[]{:S(2)}, u32[]{:S(2)}) collective-permute-start(f32[4,64]{1,0:T(4,128)S(1)} %add.151), channel_id=1, source_target_pairs={{0,16},{16,32},{32,48},{48,64},{64,80},{80,96},{96,112},{112,128},... | collective-permute-start | bytes 3080 | tf_op jit(solution)/shard_map/while/body/eval_jaxpr/ppermute | solution.py:29
  130.1 6.1 %collective-permute-start = (f32[4,64]{1,0:T(4,128)S(1)}, f32[4,64]{1,0:T(4,128)S(1)}, u32[]{:S(2)}, u32[]{:S(2)}) collective-permute-start(f32[4,64]{1,0:T(4,128)S(1)} %add.151), channel_id=1, source_target_pairs={{0,16},{16,32},{32,48},{48,64},{64,80},{80,96},{96,112},{112,128},... | collective-permute-start | bytes 3080 | tf_op jit(solution)/shard_map/while/body/eval_jaxpr/ppermute | solution.py:29
  136.5 6.1 %collective-permute-start = (f32[4,64]{1,0:T(4,128)S(1)}, f32[4,64]{1,0:T(4,128)S(1)}, u32[]{:S(2)}, u32[]{:S(2)}) collective-permute-start(f32[4,64]{1,0:T(4,128)S(1)} %add.151), channel_id=1, source_target_pairs={{0,16},{16,32},{32,48},{48,64},{64,80},{80,96},{96,112},{112,128},... | collective-permute-start | bytes 3080 | tf_op jit(solution)/shard_map/while/body/eval_jaxpr/ppermute | solution.py:29
  143.0 6.1 %collective-permute-start = (f32[4,64]{1,0:T(4,128)S(1)}, f32[4,64]{1,0:T(4,128)S(1)}, u32[]{:S(2)}, u32[]{:S(2)}) collective-permute-start(f32[4,64]{1,0:T(4,128)S(1)} %add.151), channel_id=1, source_target_pairs={{0,16},{16,32},{32,48},{48,64},{64,80},{80,96},{96,112},{112,128},... | collective-permute-start | bytes 3080 | tf_op jit(solution)/shard_map/while/body/eval_jaxpr/ppermute | solution.py:29
  149.4 6.1 %collective-permute-start = (f32[4,64]{1,0:T(4,128)S(1)}, f32[4,64]{1,0:T(4,128)S(1)}, u32[]{:S(2)}, u32[]{:S(2)}) collective-permute-start(f32[4,64]{1,0:T(4,128)S(1)} %add.151), channel_id=1, source_target_pairs={{0,16},{16,32},{32,48},{48,64},{64,80},{80,96},{96,112},{112,128},... | collective-permute-start | bytes 3080 | tf_op jit(solution)/shard_map/while/body/eval_jaxpr/ppermute | solution.py:29
  155.8 6.1 %collective-permute-start = (f32[4,64]{1,0:T(4,128)S(1)}, f32[4,64]{1,0:T(4,128)S(1)}, u32[]{:S(2)}, u32[]{:S(2)}) collective-permute-start(f32[4,64]{1,0:T(4,128)S(1)} %add.151), channel_id=1, source_target_pairs={{0,16},{16,32},{32,48},{48,64},{64,80},{80,96},{96,112},{112,128},... | collective-permute-start | bytes 3080 | tf_op jit(solution)/shard_map/while/body/eval_jaxpr/ppermute | solution.py:29
  162.3 6.1 %collective-permute-start = (f32[4,64]{1,0:T(4,128)S(1)}, f32[4,64]{1,0:T(4,128)S(1)}, u32[]{:S(2)}, u32[]{:S(2)}) collective-permute-start(f32[4,64]{1,0:T(4,128)S(1)} %add.151), channel_id=1, source_target_pairs={{0,16},{16,32},{32,48},{48,64},{64,80},{80,96},{96,112},{112,128},... | collective-permute-start | bytes 3080 | tf_op jit(solution)/shard_map/while/body/eval_jaxpr/ppermute | solution.py:29
  168.7 6.1 %collective-permute-start = (f32[4,64]{1,0:T(4,128)S(1)}, f32[4,64]{1,0:T(4,128)S(1)}, u32[]{:S(2)}, u32[]{:S(2)}) collective-permute-start(f32[4,64]{1,0:T(4,128)S(1)} %add.151), channel_id=1, source_target_pairs={{0,16},{16,32},{32,48},{48,64},{64,80},{80,96},{96,112},{112,128},... | collective-permute-start | bytes 3080 | tf_op jit(solution)/shard_map/while/body/eval_jaxpr/ppermute | solution.py:29
  175.1 6.1 %collective-permute-start = (f32[4,64]{1,0:T(4,128)S(1)}, f32[4,64]{1,0:T(4,128)S(1)}, u32[]{:S(2)}, u32[]{:S(2)}) collective-permute-start(f32[4,64]{1,0:T(4,128)S(1)} %add.151), channel_id=1, source_target_pairs={{0,16},{16,32},{32,48},{48,64},{64,80},{80,96},{96,112},{112,128},... | collective-permute-start | bytes 3080 | tf_op jit(solution)/shard_map/while/body/eval_jaxpr/ppermute | solution.py:29
  181.6 6.1 %collective-permute-start = (f32[4,64]{1,0:T(4,128)S(1)}, f32[4,64]{1,0:T(4,128)S(1)}, u32[]{:S(2)}, u32[]{:S(2)}) collective-permute-start(f32[4,64]{1,0:T(4,128)S(1)} %add.151), channel_id=1, source_target_pairs={{0,16},{16,32},{32,48},{48,64},{64,80},{80,96},{96,112},{112,128},... | collective-permute-start | bytes 3080 | tf_op jit(solution)/shard_map/while/body/eval_jaxpr/ppermute | solution.py:29
  188.0 6.1 %collective-permute-start = (f32[4,64]{1,0:T(4,128)S(1)}, f32[4,64]{1,0:T(4,128)S(1)}, u32[]{:S(2)}, u32[]{:S(2)}) collective-permute-start(f32[4,64]{1,0:T(4,128)S(1)} %add.151), channel_id=1, source_target_pairs={{0,16},{16,32},{32,48},{48,64},{64,80},{80,96},{96,112},{112,128},... | collective-permute-start | bytes 3080 | tf_op jit(solution)/shard_map/while/body/eval_jaxpr/ppermute | solution.py:29
  194.5 6.1 %collective-permute-start = (f32[4,64]{1,0:T(4,128)S(1)}, f32[4,64]{1,0:T(4,128)S(1)}, u32[]{:S(2)}, u32[]{:S(2)}) collective-permute-start(f32[4,64]{1,0:T(4,128)S(1)} %add.151), channel_id=1, source_target_pairs={{0,16},{16,32},{32,48},{48,64},{64,80},{80,96},{96,112},{112,128},... | collective-permute-start | bytes 3080 | tf_op jit(solution)/shard_map/while/body/eval_jaxpr/ppermute | solution.py:29
  200.9 6.1 %collective-permute-start = (f32[4,64]{1,0:T(4,128)S(1)}, f32[4,64]{1,0:T(4,128)S(1)}, u32[]{:S(2)}, u32[]{:S(2)}) collective-permute-start(f32[4,64]{1,0:T(4,128)S(1)} %add.151), channel_id=1, source_target_pairs={{0,16},{16,32},{32,48},{48,64},{64,80},{80,96},{96,112},{112,128},... | collective-permute-start | bytes 3080 | tf_op jit(solution)/shard_map/while/body/eval_jaxpr/ppermute | solution.py:29
  207.3 6.1 %collective-permute-start = (f32[4,64]{1,0:T(4,128)S(1)}, f32[4,64]{1,0:T(4,128)S(1)}, u32[]{:S(2)}, u32[]{:S(2)}) collective-permute-start(f32[4,64]{1,0:T(4,128)S(1)} %add.151), channel_id=1, source_target_pairs={{0,16},{16,32},{32,48},{48,64},{64,80},{80,96},{96,112},{112,128},... | collective-permute-start | bytes 3080 | tf_op jit(solution)/shard_map/while/body/eval_jaxpr/ppermute | solution.py:29
where the time goes:
time: 229 us; the launch traced here: 227 us
  matrix products  74.8 us (33%)
  waiting for transfers between devices  68.1 us (30%)
  starting transfers between devices  41.9 us (18%)
  local copies, waits for them, and re-layouts  41.2 us (18%)
    ppermute x15, waiting for transfers between devices, shifted(): return lax.ppermute(shard, axis, pairs)  62.7 us
    ppermute x15, starting transfers between devices, shifted(): return lax.ppermute(shard, axis, pairs)  29.1 us
    dot_general x16, matrix products, advance(): jnp.einsum('blij,blj->bli', inverse_now, balance, precision=precise, pref...  23.5 us
    dot_general x16, matrix products, advance(): jnp.einsum('blij,blj->bli', lower_now, earlier, precision=precise, prefer...  23.5 us
    reshape x1, local copies, waits for them, and re-layouts, on_device(): coupling.reshape(elements, lines_dev, coupling.shape[2], block_width, blo...  14.4 us
    dot_general x1, matrix products, on_device(): jnp.einsum('bklij,blj->bkli', spike_mat, inflows, precision=precise, pref...  12 us
    dot_general x1, matrix products, on_device(): jnp.einsum('elfij,elfj->eli', couple_mat, picked, precision=precise, pref...  8.9 us
    ppermute x2, starting transfers between devices, padded_2(): lax.ppermute(lax.slice_in_dim(block, 0, width, axis=dim), axis, backward)  7.82 us
  transfers between devices with their start and end apart: 19, of which 17 were waited for; matrix products, arithmetic and copies ran while one was open for 16% of the time, Pallas kernels for 0%

commit v1 on v0

v1 whole, which is shorter than its diff:
```python
import functools

import jax
import jax.numpy as jnp
from jax import lax
from jax.experimental import pallas as pl
from jax.experimental.pallas import tpu as pltpu
from jax.sharding import PartitionSpec as P

WIDTH = 64
SPAN = 16
LANES = 128
F32 = jnp.float32
BF16 = jnp.bfloat16


def iota(shape, dim):
    return lax.broadcasted_iota(jnp.int32, shape, dim)


def swap_halves(x):
    return jnp.concatenate([x[:, WIDTH:], x[:, :WIDTH]], axis=1)


def dot(a, b):
    return jnp.dot(a, b, preferred_element_type=F32)


def dot_t(a, b):
    return lax.dot_general(a, b, (((1,), (1,)), ((), ())), preferred_element_type=F32)


def split(x):
    high = x.astype(BF16)
    return high, (x - high.astype(F32)).astype(BF16)


def both(x):
    high = x.astype(BF16).astype(F32)
    return jnp.concatenate([high, x - high], axis=0).astype(BF16)


def fold(y):
    return y[:8] + y[8:]


def order_rows():
    row, col = iota((256, 256), 0), iota((256, 256), 1)
    line, i = row // WIDTH, row % WIDTH
    swapped = (i % 2) != (line % 2)
    want = 4 * (i // 2) + line + jnp.where(swapped, LANES, 0)
    return jnp.where(col == want, 1.0, 0.0).astype(BF16)


def half_mask(rows):
    return (iota((rows, LANES), 0) // WIDTH) % 2 == iota((rows, LANES), 1) // WIDTH


def paired(x, order):
    both_ways = jnp.concatenate([x, swap_halves(x)], axis=0)
    y = dot(order, both_ways)
    return jnp.where(half_mask(256), y, 0.0).astype(BF16)


def expand(c):
    s = swap_halves(c)
    low = iota(c.shape, 1) < WIDTH
    mask = half_mask(LANES)
    return (
        jnp.where(mask, jnp.where(low, c, s), 0.0),
        jnp.where(mask, jnp.where(low, s, c), 0.0),
    )


def device_map_kernel(spike_ref, out_ref, order_ref):
    b = pl.program_id(0)

    @pl.when(b == 0)
    def _():
        order_ref[...] = order_rows()

    m = paired(spike_ref[0], order_ref[...])
    low = iota((LANES, LANES), 1) < WIDTH

    @pl.when(b == 0)
    def _():
        m0, m1 = m[:LANES].astype(F32), m[LANES:].astype(F32)
        out_ref[...] = jnp.where(low, m0 + swap_halves(m0), m1 + swap_halves(m1))

    @pl.when(b > 0)
    def _():
        high, rest = split(out_ref[...])
        y = dot(m, high) + dot(m, rest)
        out_ref[...] = jnp.where(low, y[:LANES], y[LANES:])


def device_map(spike):
    blocks = spike.shape[0] // SPAN
    return pl.pallas_call(
        device_map_kernel,
        grid=(blocks,),
        in_specs=[pl.BlockSpec((1, LANES, LANES), lambda b: (SPAN * b + SPAN - 1, 0, 0))],
        out_specs=pl.BlockSpec((LANES, LANES), lambda b: (0, 0)),
        out_shape=jax.ShapeDtypeStruct((LANES, LANES), F32),
        scratch_shapes=[pltpu.VMEM((256, 256), BF16)],
        name="device_map",
    )(spike)


def product_kernel(upper_ref, own_ref, other_ref, out_ref):
    upper = upper_ref[0] > 0
    own, other = own_ref[...], other_ref[...]
    after = jnp.where(upper, own, other)
    before_h, before_l = split(jnp.where(upper, other, own))
    low = iota((LANES, LANES), 1) < WIDTH
    parts = []
    for m in expand(after):
        high, rest = split(m)
        parts.append(dot(high, before_h) + dot(rest, before_h) + dot(high, before_l))
    out_ref[...] = jnp.where(low, parts[0], parts[1])


def product(upper, own, other):
    return pl.pallas_call(
        product_kernel,
        in_specs=[
            pl.BlockSpec(memory_space=pltpu.SMEM),
            pl.BlockSpec(memory_space=pltpu.VMEM),
            pl.BlockSpec(memory_space=pltpu.VMEM),
        ],
        out_specs=pl.BlockSpec(memory_space=pltpu.VMEM),
        out_shape=jax.ShapeDtypeStruct((LANES, LANES), F32),
        name="product",
    )(upper, own, other)


def arrange_kernel(*refs):
    count = (len(refs) - 1) // 2
    order_ref = refs[-1]

    @pl.when(pl.program_id(0) == 0)
    def _():
        order_ref[...] = order_rows()

    order = order_ref[...]
    for src, dst in zip(refs[:count], refs[count : 2 * count]):
        for e in range(src.shape[0]):
            dst[e] = paired(src[e], order)


def arrange(*arrays):
    n = arrays[0].shape[0]
    step = 8
    return pl.pallas_call(
        arrange_kernel,
        grid=(n // step,),
        in_specs=[pl.BlockSpec((step, LANES, LANES), lambda e: (e, 0, 0))] * len(arrays),
        out_specs=[pl.BlockSpec((step, 256, LANES), lambda e: (e, 0, 0))] * len(arrays),
        out_shape=[jax.ShapeDtypeStruct((n, 256, LANES), BF16)] * len(arrays),
        scratch_shapes=[pltpu.VMEM((256, 256), BF16)],
        cost_estimate=pl.CostEstimate(
            flops=2 * len(arrays) * n * 256 * 256 * 128,
            bytes_accessed=len(arrays) * n * 3 * 32768,
            transcendentals=0,
        ),
        name="arrange",
    )(*arrays)


def times_blocks(x, mats):
    lhs = both(x)
    row = iota((8, LANES), 0)
    y = None
    for b, m in enumerate(mats):
        part = fold(dot_t(lhs, m))
        y = part if y is None else jnp.where(row == b, part, y)
    return y


def times_map(x, c_parts):
    lhs = both(x)
    high, rest = c_parts
    y = dot_t(lhs, high)
    return fold(y) + dot_t(lhs, rest)[:8]


def local_kernel(
    me_ref,
    code_ref,
    low_ref,
    high_ref,
    rhs_ref,
    coupling_hbm,
    lower_hbm,
    dinv_hbm,
    spike_hbm,
    t1_ref,
    t2_ref,
    t4_ref,
    g_ref,
    send_ref,
    coupling_v,
    lower_v,
    dinv_v,
    spike_v,
    vec,
    raw,
    res,
    sol,
    sems,
):
    n = rhs_ref.shape[0]
    blocks = n // SPAN
    copies = [
        pltpu.make_async_copy(coupling_hbm, coupling_v, sems.at[0]),
        pltpu.make_async_copy(lower_hbm, lower_v, sems.at[1]),
        pltpu.make_async_copy(dinv_hbm, dinv_v, sems.at[2]),
    ]
    for b in range(1, blocks):
        copies.append(
            pltpu.make_async_copy(spike_hbm.at[SPAN * b + SPAN - 1], spike_v.at[b], sems.at[2 + b])
        )
    for c in copies:
        c.start()

    code = code_ref[...].astype(BF16)
    r8, c8 = iota((8, 512), 0), iota((8, 512), 1)
    spread = jnp.where((r8 // 2 == (c8 % 256) // WIDTH) & (r8 % 2 == c8 // 256), 1.0, 0.0)
    where = lax.dot_general(
        code, spread.astype(BF16), (((0,), (0,)), ((), ())), preferred_element_type=F32
    )
    sides = (low_ref, high_ref)
    lane = iota((n, LANES), 1)
    for f in range(2):
        for p in range(2):
            lanes = slice(LANES * p, LANES * (p + 1))
            w = where[:, 256 * f + LANES * p : 256 * f + LANES * (p + 1)]
            x = jnp.zeros((n, LANES), F32)
            for side in range(2):
                for s in range(3):
                    x = jnp.where(w == float(3 * side + s), sides[side][pl.ds(s, n), lanes], x)
            top = x.astype(BF16).astype(F32)
            for h, part in enumerate((top, x - top)):
                turned = swap_halves(part)
                for q in range(2):
                    for a in range(2):
                        v = jnp.where(lane // WIDTH == a, part if a == q else turned, 0.0)
                        vec[2 * p + h, pl.ds(4 * q + 2 * f + a, n, stride=8), :] = v

    copies[0].wait()
    for e in range(n):
        for p in range(2):
            lhs = jnp.concatenate(
                [vec[2 * p, 8 * e : 8 * e + 8, :], vec[2 * p + 1, 8 * e : 8 * e + 8, :]], axis=0
            ).astype(BF16)
            raw[p, 8 * e : 8 * e + 8, :] = fold(
                dot_t(lhs, coupling_v[e, LANES * p : LANES * (p + 1), :])
            )
    even = lane % 2 == 0
    for p in range(2):
        y = None
        for a in range(2):
            acc = jnp.zeros((n, LANES), F32)
            for q in range(2):
                for f in range(2):
                    z = raw[p, pl.ds(4 * q + 2 * f + a, n, stride=8), :]
                    acc = jnp.where((lane // WIDTH == q) & (lane % 2 == f), z, acc)
            acc = acc + jnp.where(even, pltpu.roll(acc, LANES - 1, 1), pltpu.roll(acc, 1, 1))
            y = acc if a == 0 else jnp.where(even, y, acc)
        residual = rhs_ref[:, LANES * p : LANES * (p + 1)] - y
        for b in range(blocks):
            res[p, pl.ds(b, SPAN, stride=8), :] = residual[SPAN * b : SPAN * (b + 1)]

    for c in copies[1:]:
        c.wait()
    g = [None, None]
    for k in range(SPAN):
        for p in range(2):
            rows = slice(LANES * p, LANES * (p + 1))
            balance = res[p, 8 * k : 8 * k + 8, :]
            if k > 0:
                balance = balance - times_blocks(
                    g[p], [lower_v[SPAN * b + k, rows, :] for b in range(blocks)]
                )
            g[p] = times_blocks(balance, [dinv_v[SPAN * b + k, rows, :] for b in range(blocks)])
            sol[p, 8 * k : 8 * k + 8, :] = g[p]
    me = me_ref[0]
    for p in range(2):
        lanes = slice(LANES * p, LANES * (p + 1))
        for b in range(blocks):
            g_ref[SPAN * b : SPAN * (b + 1), lanes] = sol[p, pl.ds(b, SPAN, stride=8), :]
        last = sol[p, 8 * (SPAN - 1) : 8 * SPAN, :]
        out = last[0:1]
        for b in range(1, blocks):
            x = jnp.broadcast_to(out, (8, LANES))
            out = fold(dot_t(both(x), spike_v[b, lanes, :]))[0:1] + last[b : b + 1]
        w = jnp.broadcast_to(out, (8, LANES))
        levels = [w]
        for m, t_ref in ((1, t1_ref), (2, t2_ref), (4, t4_ref)):
            moved = times_map(w, split(expand(t_ref[...])[p]))
            w = jnp.where((me // m) % 2 == 0, moved, w)
            levels.append(w)
        for half in range(2):
            target = iota((8, LANES), 0) + 8 * half
            message = jnp.zeros((8, LANES), F32)
            for lev, m in enumerate((1, 2, 4, 8)):
                reach = (target // (2 * m) == me // (2 * m)) & (target // m == me // m + 1)
                message = jnp.where(reach, levels[lev], message)
            send_ref[8 * half : 8 * half + 8, lanes] = message


def local(me, code, low, high, rhs, coupling, lower, dinv, spike, t1, t2, t4):
    n = rhs.shape[0]
    blocks = n // SPAN
    vmem = pl.BlockSpec(memory_space=pltpu.VMEM)
    hbm = pl.BlockSpec(memory_space=pl.ANY)
    return pl.pallas_call(
        local_kernel,
        in_specs=[pl.BlockSpec(memory_space=pltpu.SMEM)] + [vmem] * 4 + [hbm] * 4 + [vmem] * 3,
        out_specs=[vmem, vmem],
        out_shape=[
            jax.ShapeDtypeStruct((n, 256), F32),
            jax.ShapeDtypeStruct((16, 256), F32),
        ],
        scratch_shapes=[
            pltpu.VMEM((n, 256, LANES), BF16),
            pltpu.VMEM((n, 256, LANES), BF16),
            pltpu.VMEM((n, 256, LANES), BF16),
            pltpu.VMEM((blocks, 256, LANES), BF16),
            pltpu.VMEM((4, 8 * n, LANES), F32),
            pltpu.VMEM((2, 8 * n, LANES), F32),
            pltpu.VMEM((2, 8 * SPAN, LANES), F32),
            pltpu.VMEM((2, 8 * SPAN, LANES), F32),
            pltpu.SemaphoreType.DMA((2 + blocks,)),
        ],
        compiler_params=pltpu.CompilerParams(vmem_limit_bytes=40 << 20),
        name="local",
    )(me, code, low, high, rhs, coupling, lower, dinv, spike, t1, t2, t4)


def finish_kernel(me_ref, got_ref, g_ref, t1_ref, t2_ref, t4_ref, spike_hbm, out_ref, spike_v, sem):
    n = g_ref.shape[0]
    blocks = n // SPAN
    copy = pltpu.make_async_copy(spike_hbm, spike_v, sem)
    copy.start()
    me = me_ref[0]
    source = iota((16, LANES), 0)
    flows = []
    for p in range(2):
        lanes = slice(LANES * p, LANES * (p + 1))
        got = got_ref[:, lanes]
        v = None
        for m, t_ref in ((8, None), (4, t4_ref), (2, t2_ref), (1, t1_ref)):
            from_here = (source // (2 * m) == me // (2 * m)) & (source // m + 1 == me // m)
            part = jnp.sum(jnp.where(from_here, got, 0.0), axis=0, keepdims=True)
            part = jnp.broadcast_to(part, (8, LANES))
            if v is None:
                v = part
            else:
                moved = times_map(v, split(expand(t_ref[...])[p]))
                v = jnp.where((me // m) % 2 == 1, moved, v) + part
        flows.append([v])
    copy.wait()
    for b in range(blocks):
        for p in range(2):
            lanes = slice(LANES * p, LANES * (p + 1))
            x = flows[p][b]
            lhs = both(x)
            for k in range(SPAN - 1, -1, -1):
                e = SPAN * b + k
                y = fold(dot_t(lhs, spike_v[e, lanes, :]))[0:1] + g_ref[e : e + 1, lanes]
                out_ref[e : e + 1, lanes] = y
                if k == SPAN - 1:
                    flows[p].append(jnp.broadcast_to(y, (8, LANES)))


def finish(me, got, g, t1, t2, t4, spike):
    n = g.shape[0]
    vmem = pl.BlockSpec(memory_space=pltpu.VMEM)
    return pl.pallas_call(
        finish_kernel,
        in_specs=[pl.BlockSpec(memory_space=pltpu.SMEM)]
        + [vmem] * 5
        + [pl.BlockSpec(memory_space=pl.ANY)],
        out_specs=vmem,
        out_shape=jax.ShapeDtypeStruct((n, 256), F32),
        scratch_shapes=[pltpu.VMEM((n, 256, LANES), BF16), pltpu.SemaphoreType.DMA],
        compiler_params=pltpu.CompilerParams(vmem_limit_bytes=32 << 20),
        name="finish",
    )(me, got, g, t1, t2, t4, spike)


def flip(x, axis, bit):
    count = lax.axis_size(axis)
    return lax.ppermute(x, axis, [(i, i ^ bit) for i in range(count)])


def between(x, axis):
    count = lax.axis_size(axis)
    pairs = [(i, i + 1) for i in range(1, count - 1, 2)]
    return lax.ppermute(x, axis, pairs + [(j, i) for i, j in pairs])


def on_device(rhs, previous, dinv, lower, spike, coupling, nbr_line, nbr_shift):
    n = rhs.shape[0]
    stream, cross = lax.axis_index("stream"), lax.axis_index("cross")
    me = stream.reshape(1)

    def as_it_lies(x):
        return x.reshape(n, 4, 32, LANES).transpose(0, 2, 1, 3).reshape(n, LANES, LANES)

    even = stream % 2 == 0
    first, last = previous[:1], previous[n - 1 :]
    mate = flip(jnp.where(even, last, first), "stream", 1)
    beyond = between(jnp.where(even, first, last), "stream")
    bordered = jnp.concatenate(
        [jnp.where(even, beyond, mate), previous, jnp.where(even, mate, beyond)], axis=0
    )
    far = between(bordered, "cross")
    near = flip(bordered, "cross", 1)
    low = jnp.where(cross % 2 == 0, far, near)
    high = jnp.where(cross % 2 == 0, near, far)

    line = cross * 4 + lax.broadcasted_iota(jnp.int32, nbr_line.shape, 1)
    code = (jnp.where(nbr_line > line, 3, 0) + nbr_shift).astype(F32)
    code = code.transpose(1, 2, 0).reshape(8, n)

    spike_x = as_it_lies(spike)
    own1 = device_map(spike_x)
    t1 = flip(own1, "stream", 1)
    own2 = product(me % 2, own1, t1)
    t2 = flip(own2, "stream", 2)
    own4 = product((me // 2) % 2, own2, t2)
    t4 = flip(own4, "stream", 4)
    lower_m, dinv_m, spike_m = arrange(as_it_lies(lower), as_it_lies(dinv), spike_x)
    coupling_x = (
        coupling.reshape(n, 4, 2, 32, LANES).transpose(0, 1, 3, 2, 4).reshape(n, 256, LANES)
    )
    g, send = local(me, code, low, high, rhs, coupling_x, lower_m, dinv_m, spike_m, t1, t2, t4)
    got = lax.all_to_all(send, "stream", 0, 0, tiled=True)
    return finish(me, got, g, t1, t2, t4, spike_m)


def solution(mesh):
    return jax.shard_map(
        on_device,
        mesh=mesh,
        in_specs=(
            P("stream", "cross"),
            P("stream", "cross"),
            P("stream", "cross", None),
            P("stream", "cross", None),
            P("stream", "cross", None),
            P("stream", "cross", None, None),
            P("stream", "cross", None),
            P("stream", "cross", None),
        ),
        out_specs=P("stream", "cross"),
        check_vma=False,
    )
```

time: 229 us -> 81.4 us (0.36)
  the two profiles are of different devices: /device:TPU:154 before, /device:TPU:7 now
where the time goes in v1:
time: 81.4 us; the launch traced here: 80.5 us
  Pallas kernels  34.2 us (42%)
  blocking collectives  16.3 us (20%)
  starting transfers between devices  16 us (20%)
  local copies, waits for them, and re-layouts  9.52 us (12%)
  waiting for transfers between devices  3.64 us (4%)
  other arithmetic  0.83 us (1%)
    all_to_all x1, blocking collectives, on_device(): got = lax.all_to_all(send, 'stream', 0, 0, tiled=True)  16.3 us
    pallas_call x1, Pallas kernels, local(): pl.pallas_call(local_kernel, in_specs=[pl.BlockSpec(memory_space=pltpu.SM...  11.9 us
    pallas_call x1, Pallas kernels, arrange(): pl.pallas_call(arrange_kernel, grid=(n // step,), in_specs=[pl.BlockSpec(...  11.3 us
    unnamed x25, local copies, waits for them, and re-layouts  9.5 us
    ppermute x2, starting transfers between devices, between(): return lax.ppermute(x, axis, pairs + [(j, i) for i, j in pairs])  8.15 us
    ppermute x5, starting transfers between devices, flip(): return lax.ppermute(x, axis, [(i, i ^ bit) for i in range(count)])  7.8 us
    pallas_call x1, Pallas kernels, finish(): pl.pallas_call(finish_kernel, in_specs=[pl.BlockSpec(memory_space=pltpu.S...  3.97 us
    ppermute x5, waiting for transfers between devices, flip(): return lax.ppermute(x, axis, [(i, i ^ bit) for i in range(count)])  3.63 us
  transfers between devices with their start and end apart: 7, of which 2 were waited for; matrix products, arithmetic and copies ran while one was open for 0% of the time, Pallas kernels for 23%

profile of v1, /device:TPU:7, one launch (start us, length us, event | category | flops | bytes accessed | tf_op | source)
XLA Modules:
  0.0 80.5 jit_solution(2741718680126257930)
XLA Ops:
  0.0 0.7 broadcast_select_fusion.5
  0.7 4.1 %collective-permute-start = (f32[1,256]{1,0:T(1,128)S(1)}, f32[1,256]{1,0:T(1,128)S(1)}, u32[]{:S(2)}, u32[]{:S(2)}) collective-permute-start(f32[1,256]{1,0:T(1,128)S(1)} %get-tuple-element.17), channel_id=1, source_target_pairs={{16,32},{48,64},{80,96},{112,128},{144,160},{176,192},{208,224},{3... | collective-permute-start | bytes 3080 | tf_op jit(solution)/shard_map/ppermute | solution.py:401
  4.8 0.1 collective-permute-start.1
  4.9 3.4 %device_map.1.own_ref = f32[128,128]{1,0:T(8,128)} custom-call(bf16[64,128,128]{2,1,0:T(8,128)(2,1)} %bitcast.32), custom_call_target="tpu_custom_call" | custom-call | tf_op jit(solution)/shard_map/device_map/pallas_call | solution.py:99
  8.4 0.5 collective-permute-start.4
  8.9 11.3 %arrange.1 = (bf16[64,256,128]{2,1,0:T(8,128)(2,1)}, bf16[64,256,128]{2,1,0:T(8,128)(2,1)}, bf16[64,256,128]{2,1,0:T(8,128)(2,1)}) custom-call(bf16[64,128,128]{2,1,0:T(8,128)(2,1)} %bitcast.34, bf16[64,128,128]{2,1,0:T(8,128)(2,1)} %bitcast.35, bf16[64,128,128]{2,1,0:T(8,128)(2,1)} %bitcast.33), custom_call_target="tpu_custom_call" | custom-call | flops 3221225472 | bytes 18874368 | tf_op jit(solution)/shard_map/arrange/pallas_call | solution.py:154
  20.3 1.4 %collective-permute-start.3 = (f32[66,256]{1,0:T(8,128)S(1)}, f32[66,256]{1,0:T(8,128)S(1)}, u32[]{:S(2)}, u32[]{:S(2)}) collective-permute-start(f32[66,256]{1,0:T(8,128)S(1)} %pad_maximum_fusion), channel_id=1, source_target_pairs={{0,1},{1,0},{2,3},{3,2},{4,5},{5,4},{6,7},{7,6},{8,9},{9,8},{10,11... | collective-permute-start | bytes 202760 | tf_op jit(solution)/shard_map/ppermute | solution.py:395
  21.6 4.1 %collective-permute-start.2 = (f32[66,256]{1,0:T(8,128)S(1)}, f32[66,256]{1,0:T(8,128)S(1)}, u32[]{:S(2)}, u32[]{:S(2)}) collective-permute-start(f32[66,256]{1,0:T(8,128)S(1)} %pad_maximum_fusion), channel_id=1, source_target_pairs={{1,2},{3,4},{5,6},{7,8},{9,10},{11,12},{13,14},{2,1},{4,3},{6,5},{... | collective-permute-start | bytes 202760 | tf_op jit(solution)/shard_map/ppermute | solution.py:401
  25.7 0.6 copy-done.4
  26.3 1.8 %product.2.own_ref = f32[128,128]{1,0:T(8,128)} custom-call(s32[1]{0:T(128)S(6)} %select_n.75.upper_ref, f32[128,128]{1,0:T(8,128)} %device_map.1.own_ref, f32[128,128]{1,0:T(8,128)} %copy-done.4), custom_call_target="tpu_custom_call" | custom-call | tf_op jit(solution)/shard_map/product/pallas_call | solution.py:124
  28.1 1.6 %collective-permute-start.5 = (f32[128,128]{1,0:T(8,128)}, f32[128,128]{1,0:T(8,128)S(1)}, u32[]{:S(2)}, u32[]{:S(2)}) collective-permute-start(f32[128,128]{1,0:T(8,128)} %product.2.own_ref), channel_id=1, source_target_pairs={{0,32},{16,48},{32,0},{48,16},{64,96},{80,112},{96,64},{112,80},{1... | collective-permute-start | bytes 196616 | tf_op jit(solution)/shard_map/ppermute | solution.py:395
  29.8 1.8 %collective-permute-done.5.other_ref.t2_ref = f32[128,128]{1,0:T(8,128)S(1)} collective-permute-done((f32[128,128]{1,0:T(8,128)}, f32[128,128]{1,0:T(8,128)S(1)}, u32[]{:S(2)}, u32[]{:S(2)}) %collective-permute-start.5) | collective-permute-done | bytes 65568 | tf_op jit(solution)/shard_map/ppermute | solution.py:395
  31.6 0.6 copy-done.6
  32.2 1.8 %product.3 = f32[128,128]{1,0:T(8,128)} custom-call(s32[1]{0:T(128)S(6)} %select_n.77.upper_ref, f32[128,128]{1,0:T(8,128)} %product.2.own_ref, f32[128,128]{1,0:T(8,128)} %copy-done.6), custom_call_target="tpu_custom_call" | custom-call | tf_op jit(solution)/shard_map/product/pallas_call | solution.py:124
  34.0 4.2 %collective-permute-start.6 = (f32[128,128]{1,0:T(8,128)}, f32[128,128]{1,0:T(8,128)S(1)}, u32[]{:S(2)}, u32[]{:S(2)}) collective-permute-start(f32[128,128]{1,0:T(8,128)} %product.3), channel_id=1, source_target_pairs={{0,64},{16,80},{32,96},{48,112},{64,0},{80,16},{96,32},{112,48},{1... | collective-permute-start | bytes 196616 | tf_op jit(solution)/shard_map/ppermute | solution.py:395
  38.2 1.8 %collective-permute-done.6.t4_ref = f32[128,128]{1,0:T(8,128)S(1)} collective-permute-done((f32[128,128]{1,0:T(8,128)}, f32[128,128]{1,0:T(8,128)S(1)}, u32[]{:S(2)}, u32[]{:S(2)}) %collective-permute-start.6) | collective-permute-done | bytes 65568 | tf_op jit(solution)/shard_map/ppermute | solution.py:395
  40.1 2.2 %copy-done.1 = bf16[64,4,2,4096]{3,2,1,0:T(2,128)(2,1)S(1)} copy-done((bf16[64,4,2,4096]{3,2,1,0:T(2,128)(2,1)S(1)}, bf16[64,4,2,4096]{3,2,1,0:T(2,128)(2,1)}, u32[]{:S(2)}) %copy-start.1) | copy-done | bytes 4194328
  42.2 2.2 %copy-done.2 = bf16[64,256,128]{2,1,0:T(8,128)(2,1)S(1)} copy-done((bf16[64,256,128]{2,1,0:T(8,128)(2,1)S(1)}, bf16[64,256,128]{2,1,0:T(8,128)(2,1)}, u32[]{:S(2)}) %copy-start.2) | copy-done | bytes 4194328
  44.4 2.2 %copy-done.3 = bf16[64,256,128]{2,1,0:T(8,128)(2,1)S(1)} copy-done((bf16[64,256,128]{2,1,0:T(8,128)(2,1)S(1)}, bf16[64,256,128]{2,1,0:T(8,128)(2,1)}, u32[]{:S(2)}) %copy-start.3) | copy-done | bytes 4194328
  46.6 0.8 %copy-done.5 = f32[128,128]{1,0:T(8,128)S(1)} copy-done((f32[128,128]{1,0:T(8,128)S(1)}, f32[128,128]{1,0:T(8,128)}, u32[]{:S(2)}) %copy-start.5) | copy-done | bytes 65560
  47.5 0.8 %copy-done.7 = f32[128,128]{1,0:T(8,128)S(1)} copy-done((f32[128,128]{1,0:T(8,128)S(1)}, f32[128,128]{1,0:T(8,128)}, u32[]{:S(2)}) %copy-start.7) | copy-done | bytes 65560
  48.3 11.9 %local.1 = (f32[64,256]{1,0:T(8,128)S(1)}, f32[16,256]{1,0:T(8,128)S(1)}) custom-call(s32[1]{0:T(128)} %bitcast.me_ref, f32[8,64]{1,0:T(8,128)S(1)} %bitcast.30, f32[66,256]{1,0:T(8,128)S(1)} %get-tuple-element.16.low_ref, f32[66,256]{1,0:T(8,128)S(1)} %get-tuple-element.15.high_ref, f32[64,256]{1,0:T(8,128)S(1)} %copy-done.8, ...), custom_call_target="tpu_custom_call" | custom-call | tf_op jit(solution)/shard_map/local/pallas_call | solution.py:317
  60.3 16.3 %all_to_all.11 = f32[16,1,256]{2,1,0:T(1,128)S(1)} all-to-all(f32[16,1,256]{2,1,0:T(1,128)S(1)} %copy.17), channel_id=1, replica_groups=mesh['stream'=16,'cross'=16] {'stream'}, dimensions={0} | all-to-all | bytes 32768 | tf_op jit(solution)/shard_map/all_to_all | solution.py:440
  76.5 4.0 %finish.1 = f32[64,256]{1,0:T(8,128)} custom-call(s32[1]{0:T(128)} %bitcast.me_ref, f32[16,256]{1,0:T(8,128)S(1)} %bitcast.29, f32[64,256]{1,0:T(8,128)S(1)} %get-tuple-element.14.g_ref, f32[128,128]{1,0:T(8,128)S(1)} %copy-done.5, f32[128,128]{1,0:T(8,128)S(1)} %copy-done.7, f32[128,128]{1,0:T(8,128)S(1)} %collective-permute-done.6.t4_ref, ...), custom_call_target="tpu_custom_call" | custom-call | tf_op jit(solution)/shard_map/finish/pallas_call | solution.py:380
  (29 shorter events, 0.2 us)
Async XLA Ops:
  0.7 19.5 %collective-permute-start = (f32[1,256]{1,0:T(1,128)S(1)}, f32[1,256]{1,0:T(1,128)S(1)}, u32[]{:S(2)}, u32[]{:S(2)}) collective-permute-start(f32[1,256]{1,0:T(1,128)S(1)} %get-tuple-element.17), channel_id=1, source_target_pairs={{16,32},{48,64},{80,96},{112,128},{144,160},{176,192},{208,224},{3... | collective-permute-start | bytes 3080 | tf_op jit(solution)/shard_map/ppermute | solution.py:401
  4.8 15.4 %collective-permute-start.1 = (f32[1,256]{1,0:T(1,128)S(1)}, f32[1,256]{1,0:T(1,128)S(1)}, u32[]{:S(2)}, u32[]{:S(2)}) collective-permute-start(f32[1,256]{1,0:T(1,128)S(1)} %get-tuple-element.18), channel_id=1, source_target_pairs={{0,16},{16,0},{32,48},{48,32},{64,80},{80,64},{96,112},{112,96},{1... | collective-permute-start | bytes 3080 | tf_op jit(solution)/shard_map/ppermute | solution.py:395
  8.4 17.4 %collective-permute-start.4 = (f32[128,128]{1,0:T(8,128)}, f32[128,128]{1,0:T(8,128)S(1)}, u32[]{:S(2)}, u32[]{:S(2)}) collective-permute-start(f32[128,128]{1,0:T(8,128)} %device_map.1.own_ref), channel_id=1, source_target_pairs={{0,16},{16,0},{32,48},{48,32},{64,80},{80,64},{96,112},{112,96},{1... | collective-permute-start | bytes 196616 | tf_op jit(solution)/shard_map/ppermute | solution.py:395
  8.9 11.4 %copy-start.9 = (f32[64,256]{1,0:T(8,128)S(1)}, f32[64,256]{1,0:T(8,128)}, u32[]{:S(2)}) copy-start(f32[64,256]{1,0:T(8,128)} %param.9) | copy-start | bytes 196612
  8.9 20.9 %copy-start.10 = (s32[64,4,2]{0,2,1:T(2,128)S(1)}, s32[64,4,2]{0,2,1:T(2,128)}, u32[]{:S(2)}) copy-start(s32[64,4,2]{0,2,1:T(2,128)} %param.15) | copy-start | bytes 6148
  8.9 20.9 %copy-start.11 = (s32[64,4,2]{0,2,1:T(2,128)S(1)}, s32[64,4,2]{0,2,1:T(2,128)}, u32[]{:S(2)}) copy-start(s32[64,4,2]{0,2,1:T(2,128)} %param.14) | copy-start | bytes 6148
  8.9 31.2 %copy-start.8 = (f32[64,256]{1,0:T(8,128)S(1)}, f32[64,256]{1,0:T(8,128)}, u32[]{:S(2)}) copy-start(f32[64,256]{1,0:T(8,128)} %rhs_ref.1) | copy-start | bytes 196612
  20.3 17.9 %collective-permute-start.3 = (f32[66,256]{1,0:T(8,128)S(1)}, f32[66,256]{1,0:T(8,128)S(1)}, u32[]{:S(2)}, u32[]{:S(2)}) collective-permute-start(f32[66,256]{1,0:T(8,128)S(1)} %pad_maximum_fusion), channel_id=1, source_target_pairs={{0,1},{1,0},{2,3},{3,2},{4,5},{5,4},{6,7},{7,6},{8,9},{9,8},{10,11... | collective-permute-start | bytes 202760 | tf_op jit(solution)/shard_map/ppermute | solution.py:395
  21.6 16.5 %collective-permute-start.2 = (f32[66,256]{1,0:T(8,128)S(1)}, f32[66,256]{1,0:T(8,128)S(1)}, u32[]{:S(2)}, u32[]{:S(2)}) collective-permute-start(f32[66,256]{1,0:T(8,128)S(1)} %pad_maximum_fusion), channel_id=1, source_target_pairs={{1,2},{3,4},{5,6},{7,8},{9,10},{11,12},{13,14},{2,1},{4,3},{6,5},{... | collective-permute-start | bytes 202760 | tf_op jit(solution)/shard_map/ppermute | solution.py:401
  25.7 0.6 copy-start.4
  28.1 3.5 %collective-permute-start.5 = (f32[128,128]{1,0:T(8,128)}, f32[128,128]{1,0:T(8,128)S(1)}, u32[]{:S(2)}, u32[]{:S(2)}) collective-permute-start(f32[128,128]{1,0:T(8,128)} %product.2.own_ref), channel_id=1, source_target_pairs={{0,32},{16,48},{32,0},{48,16},{64,96},{80,112},{96,64},{112,80},{1... | collective-permute-start | bytes 196616 | tf_op jit(solution)/shard_map/ppermute | solution.py:395
  31.6 0.6 copy-start.6
  34.0 6.1 %collective-permute-start.6 = (f32[128,128]{1,0:T(8,128)}, f32[128,128]{1,0:T(8,128)S(1)}, u32[]{:S(2)}, u32[]{:S(2)}) collective-permute-start(f32[128,128]{1,0:T(8,128)} %product.3), channel_id=1, source_target_pairs={{0,64},{16,80},{32,96},{48,112},{64,0},{80,16},{96,32},{112,48},{1... | collective-permute-start | bytes 196616 | tf_op jit(solution)/shard_map/ppermute | solution.py:395
  40.1 2.2 %copy-start.1 = (bf16[64,4,2,4096]{3,2,1,0:T(2,128)(2,1)S(1)}, bf16[64,4,2,4096]{3,2,1,0:T(2,128)(2,1)}, u32[]{:S(2)}) copy-start(bf16[64,4,2,4096]{3,2,1,0:T(2,128)(2,1)} %param.13) | copy-start | bytes 12582916
  42.2 2.2 %copy-start.2 = (bf16[64,256,128]{2,1,0:T(8,128)(2,1)S(1)}, bf16[64,256,128]{2,1,0:T(8,128)(2,1)}, u32[]{:S(2)}) copy-start(bf16[64,256,128]{2,1,0:T(8,128)(2,1)} %get-tuple-element.10.lower_hbm) | copy-start | bytes 12582916
  44.4 2.2 %copy-start.3 = (bf16[64,256,128]{2,1,0:T(8,128)(2,1)S(1)}, bf16[64,256,128]{2,1,0:T(8,128)(2,1)}, u32[]{:S(2)}) copy-start(bf16[64,256,128]{2,1,0:T(8,128)(2,1)} %get-tuple-element.11.dinv_hbm) | copy-start | bytes 12582916
  46.6 0.8 %copy-start.5 = (f32[128,128]{1,0:T(8,128)S(1)}, f32[128,128]{1,0:T(8,128)}, u32[]{:S(2)}) copy-start(f32[128,128]{1,0:T(8,128)} %copy-done.4) | copy-start | bytes 196612
  47.5 0.8 %copy-start.7 = (f32[128,128]{1,0:T(8,128)S(1)}, f32[128,128]{1,0:T(8,128)}, u32[]{:S(2)}) copy-start(f32[128,128]{1,0:T(8,128)} %copy-done.6) | copy-start | bytes 196612
  48.3 28.2 %copy-start = (bf16[64,256,128]{2,1,0:T(8,128)(2,1)S(1)}, bf16[64,256,128]{2,1,0:T(8,128)(2,1)}, u32[]{:S(2)}) copy-start(bf16[64,256,128]{2,1,0:T(8,128)(2,1)} %get-tuple-element.12.spike_hbm) | copy-start | bytes 12582916

commit v2 on v1

v2 whole, which is shorter than its diff:
```python
import functools

import jax
import jax.numpy as jnp
from jax import lax
from jax.experimental import pallas as pl
from jax.experimental.pallas import tpu as pltpu
from jax.sharding import PartitionSpec as P

WIDTH = 64
SPAN = 16
LANES = 128
F32 = jnp.float32
BF16 = jnp.bfloat16


def iota(shape, dim):
    return lax.broadcasted_iota(jnp.int32, shape, dim)


def swap_halves(x):
    return jnp.concatenate([x[:, WIDTH:], x[:, :WIDTH]], axis=1)


def dot(a, b):
    return jnp.dot(a, b, preferred_element_type=F32)


def dot_t(a, b):
    return lax.dot_general(a, b, (((1,), (1,)), ((), ())), preferred_element_type=F32)


def split(x):
    high = x.astype(BF16)
    return high, (x - high.astype(F32)).astype(BF16)


def both(x):
    high = x.astype(BF16).astype(F32)
    return jnp.concatenate([high, x - high], axis=0).astype(BF16)


def fold(y):
    return y[:8] + y[8:]


def order_rows():
    row, col = iota((256, 256), 0), iota((256, 256), 1)
    line, i = row // WIDTH, row % WIDTH
    swapped = (i % 2) != (line % 2)
    want = 4 * (i // 2) + line + jnp.where(swapped, LANES, 0)
    return jnp.where(col == want, 1.0, 0.0).astype(BF16)


def half_mask(rows):
    return (iota((rows, LANES), 0) // WIDTH) % 2 == iota((rows, LANES), 1) // WIDTH


def paired(x, order):
    both_ways = jnp.concatenate([x, swap_halves(x)], axis=0)
    y = dot(order, both_ways)
    return jnp.where(half_mask(256), y, 0.0).astype(BF16)


def expand(c):
    s = swap_halves(c)
    low = iota(c.shape, 1) < WIDTH
    mask = half_mask(LANES)
    return (
        jnp.where(mask, jnp.where(low, c, s), 0.0),
        jnp.where(mask, jnp.where(low, s, c), 0.0),
    )


def device_map_kernel(spike_hbm, out_ref, spike_v, sems):
    blocks = spike_v.shape[0]
    copies = [
        pltpu.make_async_copy(spike_hbm.at[SPAN * b + SPAN - 1], spike_v.at[b], sems.at[b])
        for b in range(blocks)
    ]
    for c in copies:
        c.start()
    order = order_rows()
    low = iota((LANES, LANES), 1) < WIDTH
    for b in range(blocks):
        copies[b].wait()
        m = paired(spike_v[b], order)
        if b == 0:
            m0, m1 = m[:LANES].astype(F32), m[LANES:].astype(F32)
            c = jnp.where(low, m0 + swap_halves(m0), m1 + swap_halves(m1))
        else:
            high, rest = split(c)
            y = dot(m, high) + dot(m, rest)
            c = jnp.where(low, y[:LANES], y[LANES:])
    out_ref[...] = c


ALMOST_ALL = 53 << 20
MOST = 49 << 20
VMEM = pl.BlockSpec(memory_space=pltpu.VMEM)
SMEM = pl.BlockSpec(memory_space=pltpu.SMEM)
HBM = pl.BlockSpec(memory_space=pltpu.HBM)


def device_map(spike):
    blocks = spike.shape[0] // SPAN
    return pl.pallas_call(
        device_map_kernel,
        in_specs=[HBM],
        out_specs=VMEM,
        out_shape=jax.ShapeDtypeStruct((LANES, LANES), F32),
        scratch_shapes=[
            pltpu.VMEM((blocks, LANES, LANES), BF16),
            pltpu.SemaphoreType.DMA((blocks,)),
        ],
        compiler_params=pltpu.CompilerParams(vmem_limit_bytes=ALMOST_ALL),
        name="device_map",
    )(spike)


def product_kernel(upper_ref, own_ref, other_ref, out_ref):
    upper = upper_ref[0] > 0
    own, other = own_ref[...], other_ref[...]
    after = jnp.where(upper, own, other)
    before_h, before_l = split(jnp.where(upper, other, own))
    low = iota((LANES, LANES), 1) < WIDTH
    parts = []
    for m in expand(after):
        high, rest = split(m)
        parts.append(dot(high, before_h) + dot(rest, before_h) + dot(high, before_l))
    out_ref[...] = jnp.where(low, parts[0], parts[1])


def product(upper, own, other):
    return pl.pallas_call(
        product_kernel,
        in_specs=[
            pl.BlockSpec(memory_space=pltpu.SMEM),
            pl.BlockSpec(memory_space=pltpu.VMEM),
            pl.BlockSpec(memory_space=pltpu.VMEM),
        ],
        out_specs=pl.BlockSpec(memory_space=pltpu.VMEM),
        out_shape=jax.ShapeDtypeStruct((LANES, LANES), F32),
        compiler_params=pltpu.CompilerParams(vmem_limit_bytes=4 << 20),
        name="product",
    )(upper, own, other)


def times_map(x, c_parts):
    lhs = both(x)
    high, rest = c_parts
    return fold(dot_t(lhs, high)) + dot_t(lhs, rest)[:8]


def reduce_lanes():
    row, col = iota((256, LANES), 0), iota((256, LANES), 1)
    return jnp.where(col % 2 == (row % LANES) // WIDTH, 1.0, 0.0).astype(BF16)


def own_lane():
    return iota((LANES, LANES), 0) // 4 == (iota((LANES, LANES), 1) % WIDTH) // 2


def lying_matvec(x, m, sums, own):
    prod = (m.astype(F32).reshape(16, 8, LANES) * x[None]).reshape(LANES, LANES)
    high = prod.astype(BF16)
    rest = (prod - high.astype(F32)).astype(BF16)
    z = dot(jnp.concatenate([high, rest], axis=1), sums)
    z = jnp.sum(jnp.where(own, z, 0.0).reshape(16, 8, LANES), axis=0)
    return z + pltpu.roll(z, 4, 0)


def line_rows(natural, p, q):
    lane = iota(natural.shape, 1)
    return jnp.where(lane // WIDTH == q, natural, swap_halves(natural))


def look_up(code_ref):
    code = code_ref[...].astype(BF16)
    r8, c8 = iota((8, 512), 0), iota((8, 512), 1)
    spread = jnp.where((r8 // 2 == (c8 % 256) // WIDTH) & (r8 % 2 == c8 // 256), 1.0, 0.0)
    return lax.dot_general(
        code, spread.astype(BF16), (((0,), (0,)), ((), ())), preferred_element_type=F32
    )


def residual_rows(n, where, rows_at, rhs, blocks_of, vec, raw):
    lane = iota((n, LANES), 1)
    for f in range(2):
        for p in range(2):
            w = where[:, 256 * f + LANES * p : 256 * f + LANES * (p + 1)]
            x = jnp.zeros((n, LANES), F32)
            for side in range(2):
                for s in range(3):
                    x = jnp.where(w == float(3 * side + s), rows_at(side, s, p), x)
            top = x.astype(BF16).astype(F32)
            for h, part in enumerate((top, x - top)):
                turned = swap_halves(part)
                for q in range(2):
                    for a in range(2):
                        v = jnp.where(lane // WIDTH == a, part if a == q else turned, 0.0)
                        vec[2 * p + h, pl.ds(4 * q + 2 * f + a, n, stride=8), :] = v

    for t, blocks in blocks_of:
        for p in range(2):
            lhs = jnp.concatenate(
                [vec[2 * p, 8 * t : 8 * t + 8, :], vec[2 * p + 1, 8 * t : 8 * t + 8, :]], axis=0
            ).astype(BF16)
            raw[p, 8 * t : 8 * t + 8, :] = fold(dot_t(lhs, blocks(p)))
    even = lane % 2 == 0
    lines = []
    for p in range(2):
        y = None
        for a in range(2):
            acc = jnp.zeros((n, LANES), F32)
            for q in range(2):
                for f in range(2):
                    z = raw[p, pl.ds(4 * q + 2 * f + a, n, stride=8), :]
                    acc = jnp.where((lane // WIDTH == q) & (lane % 2 == f), z, acc)
            acc = acc + jnp.where(even, pltpu.roll(acc, LANES - 1, 1), pltpu.roll(acc, 1, 1))
            y = acc if a == 0 else jnp.where(even, y, acc)
        residual = rhs[:, LANES * p : LANES * (p + 1)] - y
        for q in range(2):
            lines.append((2 * p + q, line_rows(residual, p, q)))
    return lines


def residual_kernel(code_ref, low_ref, high_ref, rhs_ref, coupling_hbm, lower_hbm, dinv_hbm, *rest):
    res, ends_ref, ends_coupling, lower_v, dinv_v, coupling_v, sides, vec, raw, sems = rest
    n = rhs_ref.shape[0]
    cuts = [0, n // 8, n // 4, n // 2, n]
    copies = {
        lo: pltpu.make_async_copy(
            coupling_hbm.at[pl.ds(lo, hi - lo)], coupling_v.at[pl.ds(lo, hi - lo)], sems.at[i]
        )
        for i, (lo, hi) in enumerate(zip(cuts, cuts[1:]))
    }
    later = [
        pltpu.make_async_copy(lower_hbm, lower_v, sems.at[4]),
        pltpu.make_async_copy(dinv_hbm, dinv_v, sems.at[5]),
    ]
    for c in list(copies.values()) + later:
        c.start()
    where = look_up(code_ref)
    ends_ref[0:1, :] = where[0:1]
    ends_ref[1:2, :] = where[n - 1 : n]
    for side, ref in enumerate((low_ref, high_ref)):
        sides[side, 0:8, :] = jnp.zeros((8, 256), F32)
        sides[side, 8 : n + 8, :] = ref[...]
        sides[side, n + 8 : n + 16, :] = jnp.zeros((8, 256), F32)

    def rows_at(side, s, p):
        return sides[side, pl.ds(7 + s, n), LANES * p : LANES * (p + 1)]

    def blocks_of():
        for e in range(n):
            if e in copies:
                copies[e].wait()
            yield e, lambda p: coupling_v[e, LANES * p : LANES * (p + 1), :]

    for line, rows in residual_rows(n, where, rows_at, rhs_ref[...], blocks_of(), vec, raw):
        res[pl.ds(line, n, stride=8), :] = rows
        res[pl.ds(line + 4, n, stride=8), :] = rows
    ends_coupling[0] = coupling_v[0]
    ends_coupling[1] = coupling_v[n - 1]
    for c in later:
        c.wait()


def residual(code, low, high, rhs, coupling, lower, dinv):
    n = rhs.shape[0]
    return pl.pallas_call(
        residual_kernel,
        in_specs=[VMEM] * 4 + [HBM] * 3,
        out_specs=[VMEM] * 5,
        out_shape=[
            jax.ShapeDtypeStruct((8 * n, LANES), F32),
            jax.ShapeDtypeStruct((2, 512), F32),
            jax.ShapeDtypeStruct((2, 256, LANES), BF16),
            jax.ShapeDtypeStruct(lower.shape, BF16),
            jax.ShapeDtypeStruct(dinv.shape, BF16),
        ],
        scratch_shapes=[
            pltpu.VMEM((n, 256, LANES), BF16),
            pltpu.VMEM((2, n + 16, 256), F32),
            pltpu.VMEM((4, 8 * n, LANES), F32),
            pltpu.VMEM((2, 8 * n, LANES), F32),
            pltpu.SemaphoreType.DMA((6,)),
        ],
        compiler_params=pltpu.CompilerParams(vmem_limit_bytes=MOST),
        cost_estimate=pl.CostEstimate(flops=10**8, bytes_accessed=4 << 20, transcendentals=0),
        name="residual",
    )(code, low, high, rhs, coupling, lower, dinv)


def edge_terms(t, code, edge, blocks):
    row, lane = iota((8, LANES), 0), iota((8, LANES), 1)
    q, f, a = row // 4, (row // 2) % 2, row % 2
    lines = jnp.zeros((8, LANES), F32)
    for p in range(2):
        lanes = slice(LANES * p, LANES * (p + 1))
        below = jnp.broadcast_to(edge[2 * t : 2 * t + 1, lanes], (8, LANES))
        above = jnp.broadcast_to(edge[2 * t + 1 : 2 * t + 2, lanes], (8, LANES))
        w = jnp.where(f == 0, code[t : t + 1, lanes], code[t : t + 1, 256 + LANES * p : 256 + LANES * (p + 1)])
        x = jnp.where(w == 2.0 * t, below, jnp.where(w == 3.0 + 2.0 * t, above, 0.0))
        x = jnp.where(lane // WIDTH == a, jnp.where(a == q, x, swap_halves(x)), 0.0)
        y = fold(dot_t(both(x), blocks(p)))
        y = jnp.where((lane // WIDTH == q) & (lane % 2 == f), y, 0.0)
        y = y + jnp.where(lane % 2 == 0, pltpu.roll(y, LANES - 1, 1), pltpu.roll(y, 1, 1))
        y = jnp.sum(jnp.where(lane % 2 == a, y, 0.0), axis=0, keepdims=True)
        y = jnp.broadcast_to(y, (8, LANES))
        for h in range(2):
            lines = jnp.where(row % 4 == 2 * p + h, line_rows(y, p, h), lines)
    return lines


def chain_kernel(
    res, ends_ref, edge_ref, coupling_ref, lower_ref, dinv_ref, spike_hbm, g_ref, out_ref, sol, spike_v, sems
):
    n = g_ref.shape[0]
    blocks = n // SPAN
    ends = (0, n - 1)
    spike_copies = [
        pltpu.make_async_copy(spike_hbm.at[SPAN * b + SPAN - 1], spike_v.at[b], sems.at[b])
        for b in range(1, blocks)
    ]
    for c in spike_copies:
        c.start()
    code, edge = ends_ref[...], edge_ref[...]
    terms = [
        edge_terms(t, code, edge, lambda p, t=t: coupling_ref[t, LANES * p : LANES * (p + 1), :])
        for t in range(2)
    ]
    sums, own = reduce_lanes(), own_lane()
    g = [None] * blocks
    for k in range(SPAN):
        for b in range(blocks):
            e = SPAN * b + k
            balance = res[8 * e : 8 * e + 8, :]
            if e in ends:
                balance = balance - terms[ends.index(e)]
            if k > 0:
                balance = balance - lying_matvec(g[b], lower_ref[e], sums, own)
            g[b] = lying_matvec(balance, dinv_ref[e], sums, own)
            sol[8 * e : 8 * e + 8, :] = g[b]
    for c in spike_copies:
        c.wait()
    out = g[0]
    for b in range(1, blocks):
        out = lying_matvec(out, spike_v[b], sums, own) + g[b]
    out_ref[...] = out
    lane = iota((n, LANES), 1)
    for p in range(2):
        g_ref[:, LANES * p : LANES * (p + 1)] = jnp.where(
            lane < WIDTH, sol[pl.ds(2 * p, n, stride=8), :], sol[pl.ds(2 * p + 1, n, stride=8), :]
        )


def chain(res, ends, edge, coupling, lower, dinv, spike):
    n = lower.shape[0]
    blocks = n // SPAN
    return pl.pallas_call(
        chain_kernel,
        in_specs=[VMEM] * 6 + [HBM],
        out_specs=[VMEM, VMEM],
        out_shape=[
            jax.ShapeDtypeStruct((n, 256), F32),
            jax.ShapeDtypeStruct((8, LANES), F32),
        ],
        scratch_shapes=[
            pltpu.VMEM((8 * n, LANES), F32),
            pltpu.VMEM((blocks, LANES, LANES), BF16),
            pltpu.SemaphoreType.DMA((blocks,)),
        ],
        compiler_params=pltpu.CompilerParams(vmem_limit_bytes=MOST),
        cost_estimate=pl.CostEstimate(flops=10**9, bytes_accessed=4 << 20, transcendentals=0),
        name="chain",
    )(res, ends, edge, coupling, lower, dinv, spike)


def outflow_kernel(me_ref, out_ref, t1_ref, t2_ref, t4_ref, send_ref):
    me = me_ref[0]
    out = out_ref[...]
    for p in range(2):
        lanes = slice(LANES * p, LANES * (p + 1))
        w = jnp.where(iota((1, LANES), 1) < WIDTH, out[2 * p : 2 * p + 1], out[2 * p + 1 : 2 * p + 2])
        w = jnp.broadcast_to(w, (8, LANES))
        levels = [w]
        for m, t_ref in ((1, t1_ref), (2, t2_ref), (4, t4_ref)):
            moved = times_map(w, split(expand(t_ref[...])[p]))
            w = jnp.where((me // m) % 2 == 0, moved, w)
            levels.append(w)
        for half in range(2):
            target = iota((8, LANES), 0) + 8 * half
            message = jnp.zeros((8, LANES), F32)
            for lev, m in enumerate((1, 2, 4, 8)):
                reach = (target // (2 * m) == me // (2 * m)) & (target // m == me // m + 1)
                message = jnp.where(reach, levels[lev], message)
            send_ref[8 * half : 8 * half + 8, lanes] = message


def outflow(me, out, t1, t2, t4):
    return pl.pallas_call(
        outflow_kernel,
        in_specs=[SMEM] + [VMEM] * 4,
        out_specs=VMEM,
        out_shape=jax.ShapeDtypeStruct((16, 256), F32),
        compiler_params=pltpu.CompilerParams(vmem_limit_bytes=4 << 20),
        name="outflow",
    )(me, out, t1, t2, t4)


def finish_kernel(me_ref, got_ref, g_ref, t1_ref, t2_ref, t4_ref, spike_ref, out_ref, raw):
    n = g_ref.shape[0]
    blocks = n // SPAN
    me = me_ref[0]
    source = iota((16, LANES), 0)
    pairs = []
    for p in range(2):
        lanes = slice(LANES * p, LANES * (p + 1))
        got = got_ref[:, lanes]
        v = None
        for m, t_ref in ((8, None), (4, t4_ref), (2, t2_ref), (1, t1_ref)):
            from_here = (source // (2 * m) == me // (2 * m)) & (source // m + 1 == me // m)
            part = jnp.sum(jnp.where(from_here, got, 0.0), axis=0, keepdims=True)
            part = jnp.broadcast_to(part, (8, LANES))
            if v is None:
                v = part
            else:
                moved = times_map(v, split(expand(t_ref[...])[p]))
                v = jnp.where((me // m) % 2 == 1, moved, v) + part
        pairs.append(v)
    row, lane = iota((8, LANES), 0), iota((8, LANES), 1)

    def lines_of(pair):
        rows = [line_rows(pair[l // 2], l // 2, l % 2) for l in range(4)]
        x = rows[0]
        for l in range(1, 4):
            x = jnp.where(row % 4 == l, rows[l], x)
        return x

    sums, own = reduce_lanes(), own_lane()
    x = lines_of(pairs)
    step = 2
    for b in range(blocks):
        lhs = both(jnp.where(row // 4 == lane // WIDTH, x, 0.0))
        if b + 1 < blocks:
            e = SPAN * b + SPAN - 1
            last = [
                jnp.broadcast_to(g_ref[e : e + 1, LANES * p : LANES * (p + 1)], (8, LANES))
                for p in range(2)
            ]
            x = lying_matvec(x, spike_ref[e], sums, own) + lines_of(last)
        for k in range(0, SPAN, step):
            e = SPAN * b + k
            y = fold(dot_t(lhs, spike_ref[e : e + step].reshape(step * LANES, LANES)))
            for t in range(step):
                raw[8 * (e + t) : 8 * (e + t) + 8, :] = y[:, LANES * t : LANES * (t + 1)]
    lane_n = iota((n, LANES), 1)
    parts = []
    for a in range(2):
        acc = jnp.zeros((n, LANES), F32)
        for l in range(4):
            acc = jnp.where(lane_n % 4 == l, raw[pl.ds(4 * a + l, n, stride=8), :], acc)
        parts.append(acc)
    y = jnp.concatenate(parts, axis=1)
    src, dst = iota((256, 256), 0), iota((256, 256), 1)
    want = LANES * (dst % 2) + 4 * ((dst % WIDTH) // 2) + dst // WIDTH
    order = jnp.where(src == want, 1.0, 0.0).astype(BF16)
    high, rest = split(y)
    out_ref[...] = dot(high, order) + dot(rest, order) + g_ref[...]


def finish(me, got, g, t1, t2, t4, spike):
    n = g.shape[0]
    vmem = pl.BlockSpec(memory_space=pltpu.VMEM)
    return pl.pallas_call(
        finish_kernel,
        in_specs=[pl.BlockSpec(memory_space=pltpu.SMEM)] + [vmem] * 6,
        out_specs=vmem,
        out_shape=jax.ShapeDtypeStruct((n, 256), F32),
        scratch_shapes=[pltpu.VMEM((8 * n, LANES), F32)],
        compiler_params=pltpu.CompilerParams(vmem_limit_bytes=4 << 20),
        name="finish",
    )(me, got, g, t1, t2, t4, spike)


def flip(x, axis, bit):
    count = lax.axis_size(axis)
    return lax.ppermute(x, axis, [(i, i ^ bit) for i in range(count)])


def between(x, axis):
    count = lax.axis_size(axis)
    pairs = [(i, i + 1) for i in range(1, count - 1, 2)]
    return lax.ppermute(x, axis, pairs + [(j, i) for i, j in pairs])


def on_device(rhs, previous, dinv, lower, spike, coupling, nbr_line, nbr_shift):
    n = rhs.shape[0]
    stream, cross = lax.axis_index("stream"), lax.axis_index("cross")
    me = stream.reshape(1)

    def as_it_lies(x):
        return x.reshape(n, 4, 32, LANES).transpose(0, 2, 1, 3).reshape(n, LANES, LANES)

    far = between(previous, "cross")
    near = flip(previous, "cross", 1)
    low = jnp.where(cross % 2 == 0, far, near)
    high = jnp.where(cross % 2 == 0, near, far)
    even = stream % 2 == 0
    first = jnp.concatenate([low[:1], high[:1]], axis=0)
    last = jnp.concatenate([low[n - 1 :], high[n - 1 :]], axis=0)
    to_mate, to_beyond = jnp.where(even, last, first), jnp.where(even, first, last)
    spike_x = as_it_lies(spike)
    own1 = device_map(spike_x)
    t1 = flip(own1, "stream", 1)
    beyond = between(to_beyond, "stream")
    mate = flip(to_mate, "stream", 1)
    mate, own1, t1 = lax.optimization_barrier((mate, own1, t1))
    edge = jnp.concatenate([jnp.where(even, beyond, mate), jnp.where(even, mate, beyond)], axis=0)
    own2 = product(me % 2, own1, t1)
    t2 = flip(own2, "stream", 2)
    low, own2 = lax.optimization_barrier((low, own2))

    line = cross * 4 + lax.broadcasted_iota(jnp.int32, nbr_line.shape, 1)
    code = (jnp.where(nbr_line > line, 3, 0) + nbr_shift).astype(F32)
    code = code.transpose(1, 2, 0).reshape(8, n)
    coupling_x = (
        coupling.reshape(n, 4, 2, 32, LANES).transpose(0, 1, 3, 2, 4).reshape(n, 256, LANES)
    )
    res, ends, ends_coupling, lower_v, dinv_v = residual(
        code, low, high, rhs, coupling_x, as_it_lies(lower), as_it_lies(dinv)
    )
    res, own2, t2 = lax.optimization_barrier((res, own2, t2))
    own4 = product((me // 2) % 2, own2, t2)
    t4 = flip(own4, "stream", 4)
    g, out = chain(res, ends, edge, ends_coupling, lower_v, dinv_v, spike_x)
    send = outflow(me, out, t1, t2, t4)
    got = lax.all_to_all(send, "stream", 0, 0, tiled=True)
    return finish(me, got, g, t1, t2, t4, spike_x)


def solution(mesh):
    return jax.shard_map(
        on_device,
        mesh=mesh,
        in_specs=(
            P("stream", "cross"),
            P("stream", "cross"),
            P("stream", "cross", None),
            P("stream", "cross", None),
            P("stream", "cross", None),
            P("stream", "cross", None, None),
            P("stream", "cross", None),
            P("stream", "cross", None),
        ),
        out_specs=P("stream", "cross"),
        check_vma=False,
    )
```

time: 81.4 us -> 47 us (0.58)
  Pallas kernels: 34.2 us -> 16.6 us
  local copies, waits for them, and re-layouts: 9.52 us -> 0.05 us
  blocking collectives: 16.3 us -> 11.8 us
  waiting for transfers between devices: 3.64 us -> 0.02 us
  starting transfers between devices: 16 us -> 18 us
    pallas_call x3 -> x4, Pallas kernels: 26.7 us -> 13.7 us  [the longest x1 6.4 us: chain(): pl.pallas_call(chain_kernel, in_specs=[VMEM] * 6 + [HBM], out_specs=[VMEM...]
    unnamed x25 -> x9, local copies, waits for them, and re-layouts: 9.5 us -> 0.02 us
    all_to_all x1, blocking collectives: 16.3 us -> 11.8 us  [on_device(): got = lax.all_to_all(send, 'stream', 0, 0, tiled=True)]
    ppermute x5, waiting for transfers between devices: 3.63 us -> 0.01 us  [flip(): return lax.ppermute(x, axis, [(i, i ^ bit) for i in range(count)])]
    pallas_call x2, Pallas kernels: 3.51 us -> 0.52 us  [product(): pl.pallas_call(product_kernel, in_specs=[pl.BlockSpec(memory_space=pltpu....]
    ppermute x5, starting transfers between devices: 7.8 us -> 10.4 us  [flip(): return lax.ppermute(x, axis, [(i, i ^ bit) for i in range(count)])]
    pallas_call x1, Pallas kernels: 3.97 us -> 2.35 us  [finish(): pl.pallas_call(finish_kernel, in_specs=[pl.BlockSpec(memory_space=pltpu.S...]
  transfers between devices with their start and end apart: 7 -> 7, of which waited for: 2 -> 0; matrix products, arithmetic and copies ran while one was open for 0% -> 0% of each run, Pallas kernels for 23% -> 28%
where the time goes in v2:
time: 47 us; the launch traced here: 46.7 us
  starting transfers between devices  18 us (38%)
  Pallas kernels  16.6 us (35%)
  blocking collectives  11.8 us (25%)
    all_to_all x1, blocking collectives, on_device(): got = lax.all_to_all(send, 'stream', 0, 0, tiled=True)  11.8 us
    ppermute x5, starting transfers between devices, flip(): return lax.ppermute(x, axis, [(i, i ^ bit) for i in range(count)])  10.4 us
    ppermute x2, starting transfers between devices, between(): return lax.ppermute(x, axis, pairs + [(j, i) for i, j in pairs])  7.51 us
    pallas_call x1, Pallas kernels, chain(): pl.pallas_call(chain_kernel, in_specs=[VMEM] * 6 + [HBM], out_specs=[VMEM...  6.4 us
    pallas_call x1, Pallas kernels, residual(): pl.pallas_call(residual_kernel, in_specs=[VMEM] * 4 + [HBM] * 3, out_spec...  4.21 us
    pallas_call x1, Pallas kernels, device_map(): pl.pallas_call(device_map_kernel, in_specs=[HBM], out_specs=VMEM, out_sha...  2.37 us
    pallas_call x1, Pallas kernels, finish(): pl.pallas_call(finish_kernel, in_specs=[pl.BlockSpec(memory_space=pltpu.S...  2.35 us
  transfers between devices with their start and end apart: 7, of which 0 were waited for; matrix products, arithmetic and copies ran while one was open for 0% of the time, Pallas kernels for 28%

profile of v2, /device:TPU:7, one launch (start us, length us, event | category | flops | bytes accessed | tf_op | source)
XLA Modules:
  0.0 46.7 jit_solution(12846741550704065047)
XLA Ops:
  0.0 1.4 %collective-permute-start.1 = (f32[64,256]{1,0:T(8,128)}, f32[64,256]{1,0:T(8,128)S(1)}, u32[]{:S(2)}, u32[]{:S(2)}) collective-permute-start(f32[64,256]{1,0:T(8,128)} %param.9), channel_id=1, source_target_pairs={{0,1},{1,0},{2,3},{3,2},{4,5},{5,4},{6,7},{7,6},{8,9},{9,8},{10,11... | collective-permute-start | bytes 196616 | tf_op jit(solution)/shard_map/ppermute | solution.py:490
  1.4 4.1 %collective-permute-start = (f32[64,256]{1,0:T(8,128)}, f32[64,256]{1,0:T(8,128)S(1)}, u32[]{:S(2)}, u32[]{:S(2)}) collective-permute-start(f32[64,256]{1,0:T(8,128)} %param.9), channel_id=1, source_target_pairs={{1,2},{3,4},{5,6},{7,8},{9,10},{11,12},{13,14},{2,1},{4,3},{6,5},{... | collective-permute-start | bytes 196616 | tf_op jit(solution)/shard_map/ppermute | solution.py:496
  5.5 2.4 %device_map.1.own_ref = f32[128,128]{1,0:T(8,128)S(1)} custom-call(bf16[64,128,128]{2,1,0:T(8,128)(2,1)} %bitcast.28), custom_call_target="tpu_custom_call" | custom-call | tf_op jit(solution)/shard_map/device_map/pallas_call | solution.py:107
  7.8 1.3 %collective-permute-start.3 = (f32[128,128]{1,0:T(8,128)S(1)}, f32[128,128]{1,0:T(8,128)S(1)}, u32[]{:S(2)}, u32[]{:S(2)}) collective-permute-start(f32[128,128]{1,0:T(8,128)S(1)} %device_map.1.own_ref), channel_id=1, source_target_pairs={{0,16},{16,0},{32,48},{48,32},{64,80},{80,64},{96,112},{112,96},{1... | collective-permute-start | bytes 196616 | tf_op jit(solution)/shard_map/ppermute | solution.py:490
  9.2 0.0 collective-permute-done.1
  9.2 0.0 collective-permute-done
  9.2 1.7 %collective-permute-start.2 = (f32[2,256]{1,0:T(2,128)S(1)}, f32[2,256]{1,0:T(2,128)S(1)}, u32[]{:S(2)}, u32[]{:S(2)}) collective-permute-start(f32[2,256]{1,0:T(2,128)S(1)} %get-tuple-element.44), channel_id=1, source_target_pairs={{0,16},{16,0},{32,48},{48,32},{64,80},{80,64},{96,112},{112,96},{1... | collective-permute-start | bytes 6152 | tf_op jit(solution)/shard_map/ppermute | solution.py:490
  11.0 0.0 copy-done.2
  11.0 0.1 fusion.1
  11.0 3.4 %collective-permute-start.5 = (f32[2,256]{1,0:T(2,128)S(1)}, f32[2,256]{1,0:T(2,128)S(1)}, u32[]{:S(2)}, u32[]{:S(2)}) collective-permute-start(f32[2,256]{1,0:T(2,128)S(1)} %get-tuple-element.43), channel_id=1, source_target_pairs={{16,32},{48,64},{80,96},{112,128},{144,160},{176,192},{208,224},{3... | collective-permute-start | bytes 6152 | tf_op jit(solution)/shard_map/ppermute | solution.py:496
  14.5 0.0 collective-permute-done.3.other_ref.t1_ref
  14.5 0.0 collective-permute-done.2
  14.5 0.3 product.2.own_ref
  14.8 1.7 %collective-permute-start.4 = (f32[128,128]{1,0:T(8,128)S(1)}, f32[128,128]{1,0:T(8,128)S(1)}, u32[]{:S(2)}, u32[]{:S(2)}) collective-permute-start(f32[128,128]{1,0:T(8,128)S(1)} %product.2.own_ref), channel_id=1, source_target_pairs={{0,32},{16,48},{32,0},{48,16},{64,96},{80,112},{96,64},{112,80},{1... | collective-permute-start | bytes 196616 | tf_op jit(solution)/shard_map/ppermute | solution.py:490
  16.5 4.2 %residual.1 = (f32[512,128]{1,0:T(8,128)S(1)}, f32[2,512]{1,0:T(2,128)S(1)}, bf16[2,256,128]{2,1,0:T(8,128)(2,1)S(1)}, bf16[64,128,128]{2,1,0:T(8,128)(2,1)S(1)}, bf16[64,128,128]{2,1,0:T(8,128)(2,1)S(1)}) custom-call(f32[8,64]{1,0:T(8,128)S(1)} %bitcast.33, f32[64,256]{1,0:T(8,128)S(1)} %get-tuple-element.22.low_ref, ...), custom_call_target="tpu_custom_call" | custom-call | flops 100000000 | bytes 4194304 | tf_op jit(solution)/shard_map/residual/pallas_call | solution.py:272
  20.7 0.0 collective-permute-done.5
  20.8 0.0 collective-permute-done.4.other_ref.t2_ref
  20.8 0.3 product.3
  21.0 4.3 %collective-permute-start.6 = (f32[128,128]{1,0:T(8,128)S(1)}, f32[128,128]{1,0:T(8,128)S(1)}, u32[]{:S(2)}, u32[]{:S(2)}) collective-permute-start(f32[128,128]{1,0:T(8,128)S(1)} %product.3), channel_id=1, source_target_pairs={{0,64},{16,80},{32,96},{48,112},{64,0},{80,16},{96,32},{112,48},{1... | collective-permute-start | bytes 196616 | tf_op jit(solution)/shard_map/ppermute | solution.py:490
  25.3 6.4 %chain.1 = (f32[64,256]{1,0:T(8,128)S(1)}, f32[8,128]{1,0:T(8,128)S(1)}) custom-call(f32[512,128]{1,0:T(8,128)S(1)} %get-tuple-element.25.res, f32[2,512]{1,0:T(2,128)S(1)} %get-tuple-element.26.ends_ref, f32[4,256]{1,0:T(4,128)S(1)} %pad_maximum_fusion.edge_ref, bf16[2,256,128]{2,1,0:T(8,128)(2,1)S(1)} %get-tuple-element.28.coupling_ref, ...), custom_call_target="tpu_custom_call" | custom-call | flops 1000000000 | bytes 4194304 | tf_op jit(solution)/shard_map/chain/pallas_call | solution.py:362
  31.7 0.0 collective-permute-done.6.t4_ref
  31.8 0.7 %outflow.1 = f32[16,256]{1,0:T(8,128)S(1)} custom-call(s32[1]{0:T(128)} %bitcast.me_ref, f32[8,128]{1,0:T(8,128)S(1)} %get-tuple-element.31.out_ref, f32[128,128]{1,0:T(8,128)S(1)} %collective-permute-done.3.other_ref.t1_ref, f32[128,128]{1,0:T(8,128)S(1)} %collective-permute-done.4.other_ref.t2_ref, f32[128,128]{1,0:T(8,128)S(1)} %collective-permute-done.6.t4_ref), custom_call_target="tpu_custom_call" | custom-call | tf_op jit(solution)/shard_map/outflow/pallas_call | solution.py:403
  32.5 11.8 %all_to_all.11 = f32[16,1,256]{2,1,0:T(1,128)S(1)} all-to-all(f32[16,1,256]{2,1,0:T(1,128)S(1)} %copy.17), channel_id=1, replica_groups=mesh['stream'=16,'cross'=16] {'stream'}, dimensions={0} | all-to-all | bytes 32768 | tf_op jit(solution)/shard_map/all_to_all | solution.py:540
  44.3 2.4 %finish.1 = f32[64,256]{1,0:T(8,128)} custom-call(s32[1]{0:T(128)} %bitcast.me_ref, f32[16,256]{1,0:T(8,128)S(1)} %bitcast.31, f32[64,256]{1,0:T(8,128)S(1)} %get-tuple-element.34.g_ref, f32[128,128]{1,0:T(8,128)S(1)} %collective-permute-done.3.other_ref.t1_ref, f32[128,128]{1,0:T(8,128)S(1)} %collective-permute-done.4.other_ref.t2_ref, ...), custom_call_target="tpu_custom_call" | custom-call | tf_op jit(solution)/shard_map/finish/pallas_call | solution.py:477
  (15 shorter events, 0.1 us)
Async XLA Ops:
  0.0 11.0 %copy-start.2 = (s32[64,4,2]{0,2,1:T(2,128)S(1)}, s32[64,4,2]{0,2,1:T(2,128)}, u32[]{:S(2)}) copy-start(s32[64,4,2]{0,2,1:T(2,128)} %param.15) | copy-start | bytes 6148
  0.0 11.0 %copy-start.3 = (s32[64,4,2]{0,2,1:T(2,128)S(1)}, s32[64,4,2]{0,2,1:T(2,128)}, u32[]{:S(2)}) copy-start(s32[64,4,2]{0,2,1:T(2,128)} %param.14) | copy-start | bytes 6148
  0.0 16.5 %copy-start.1 = (f32[64,256]{1,0:T(8,128)S(1)}, f32[64,256]{1,0:T(8,128)}, u32[]{:S(2)}) copy-start(f32[64,256]{1,0:T(8,128)} %rhs_ref.1) | copy-start | bytes 196612
  0.0 9.2 %collective-permute-start.1 = (f32[64,256]{1,0:T(8,128)}, f32[64,256]{1,0:T(8,128)S(1)}, u32[]{:S(2)}, u32[]{:S(2)}) collective-permute-start(f32[64,256]{1,0:T(8,128)} %param.9), channel_id=1, source_target_pairs={{0,1},{1,0},{2,3},{3,2},{4,5},{5,4},{6,7},{7,6},{8,9},{9,8},{10,11... | collective-permute-start | bytes 196616 | tf_op jit(solution)/shard_map/ppermute | solution.py:490
  1.4 7.8 %collective-permute-start = (f32[64,256]{1,0:T(8,128)}, f32[64,256]{1,0:T(8,128)S(1)}, u32[]{:S(2)}, u32[]{:S(2)}) collective-permute-start(f32[64,256]{1,0:T(8,128)} %param.9), channel_id=1, source_target_pairs={{1,2},{3,4},{5,6},{7,8},{9,10},{11,12},{13,14},{2,1},{4,3},{6,5},{... | collective-permute-start | bytes 196616 | tf_op jit(solution)/shard_map/ppermute | solution.py:496
  7.8 6.6 %collective-permute-start.3 = (f32[128,128]{1,0:T(8,128)S(1)}, f32[128,128]{1,0:T(8,128)S(1)}, u32[]{:S(2)}, u32[]{:S(2)}) collective-permute-start(f32[128,128]{1,0:T(8,128)S(1)} %device_map.1.own_ref), channel_id=1, source_target_pairs={{0,16},{16,0},{32,48},{48,32},{64,80},{80,64},{96,112},{112,96},{1... | collective-permute-start | bytes 196616 | tf_op jit(solution)/shard_map/ppermute | solution.py:490
  9.2 5.3 %collective-permute-start.2 = (f32[2,256]{1,0:T(2,128)S(1)}, f32[2,256]{1,0:T(2,128)S(1)}, u32[]{:S(2)}, u32[]{:S(2)}) collective-permute-start(f32[2,256]{1,0:T(2,128)S(1)} %get-tuple-element.44), channel_id=1, source_target_pairs={{0,16},{16,0},{32,48},{48,32},{64,80},{80,64},{96,112},{112,96},{1... | collective-permute-start | bytes 6152 | tf_op jit(solution)/shard_map/ppermute | solution.py:490
  11.0 9.7 %collective-permute-start.5 = (f32[2,256]{1,0:T(2,128)S(1)}, f32[2,256]{1,0:T(2,128)S(1)}, u32[]{:S(2)}, u32[]{:S(2)}) collective-permute-start(f32[2,256]{1,0:T(2,128)S(1)} %get-tuple-element.43), channel_id=1, source_target_pairs={{16,32},{48,64},{80,96},{112,128},{144,160},{176,192},{208,224},{3... | collective-permute-start | bytes 6152 | tf_op jit(solution)/shard_map/ppermute | solution.py:496
  14.8 6.0 %collective-permute-start.4 = (f32[128,128]{1,0:T(8,128)S(1)}, f32[128,128]{1,0:T(8,128)S(1)}, u32[]{:S(2)}, u32[]{:S(2)}) collective-permute-start(f32[128,128]{1,0:T(8,128)S(1)} %product.2.own_ref), channel_id=1, source_target_pairs={{0,32},{16,48},{32,0},{48,16},{64,96},{80,112},{96,64},{112,80},{1... | collective-permute-start | bytes 196616 | tf_op jit(solution)/shard_map/ppermute | solution.py:490
  21.0 10.7 %collective-permute-start.6 = (f32[128,128]{1,0:T(8,128)S(1)}, f32[128,128]{1,0:T(8,128)S(1)}, u32[]{:S(2)}, u32[]{:S(2)}) collective-permute-start(f32[128,128]{1,0:T(8,128)S(1)} %product.3), channel_id=1, source_target_pairs={{0,64},{16,80},{32,96},{48,112},{64,0},{80,16},{96,32},{112,48},{1... | collective-permute-start | bytes 196616 | tf_op jit(solution)/shard_map/ppermute | solution.py:490
  25.3 19.0 %copy-start = (bf16[64,4,4096]{2,1,0:T(4,128)(2,1)S(1)}, bf16[64,4,4096]{2,1,0:T(4,128)(2,1)}, u32[]{:S(2)}) copy-start(bf16[64,4,4096]{2,1,0:T(4,128)(2,1)} %param.12) | copy-start | bytes 6291460

commit v3 on v2

--- a/solution.py
+++ b/solution.py
@@ -72,7 +72,7 @@
     )
 
 
-def device_map_kernel(spike_hbm, out_ref, spike_v, sems):
+def device_map_kernel(spike_hbm, out_ref, after_ref, spike_v, sems):
     blocks = spike_v.shape[0]
     copies = [
         pltpu.make_async_copy(spike_hbm.at[SPAN * b + SPAN - 1], spike_v.at[b], sems.at[b])
@@ -82,17 +82,23 @@
         c.start()
     order = order_rows()
     low = iota((LANES, LANES), 1) < WIDTH
-    for b in range(blocks):
+    total = None
+    for b in range(blocks - 1, -1, -1):
         copies[b].wait()
         m = paired(spike_v[b], order)
-        if b == 0:
-            m0, m1 = m[:LANES].astype(F32), m[LANES:].astype(F32)
-            c = jnp.where(low, m0 + swap_halves(m0), m1 + swap_halves(m1))
+        m0, m1 = m[:LANES].astype(F32), m[LANES:].astype(F32)
+        c = jnp.where(low, m0 + swap_halves(m0), m1 + swap_halves(m1))
+        if total is None:
+            total = c
         else:
-            high, rest = split(c)
-            y = dot(m, high) + dot(m, rest)
-            c = jnp.where(low, y[:LANES], y[LANES:])
-    out_ref[...] = c
+            before, parts = c.astype(BF16), []
+            for after in expand(total):
+                high, rest = split(after)
+                parts.append(dot(high, before) + dot(rest, before))
+            total = jnp.where(low, parts[0], parts[1])
+        if b > 0:
+            after_ref[b - 1] = total
+    out_ref[...] = total
 
 
 ALMOST_ALL = 53 << 20
@@ -107,8 +113,11 @@
     return pl.pallas_call(
         device_map_kernel,
         in_specs=[HBM],
-        out_specs=VMEM,
-        out_shape=jax.ShapeDtypeStruct((LANES, LANES), F32),
+        out_specs=[VMEM] * 2,
+        out_shape=[
+            jax.ShapeDtypeStruct((LANES, LANES), F32),
+            jax.ShapeDtypeStruct((blocks - 1, LANES, LANES), F32),
+        ],
         scratch_shapes=[
             pltpu.VMEM((blocks, LANES, LANES), BF16),
             pltpu.SemaphoreType.DMA((blocks,)),
@@ -118,7 +127,7 @@
     )(spike)
 
 
-def product_kernel(upper_ref, own_ref, other_ref, out_ref):
+def multiply(upper_ref, own_ref, other_ref):
     upper = upper_ref[0] > 0
     own, other = own_ref[...], other_ref[...]
     after = jnp.where(upper, own, other)
@@ -128,7 +137,11 @@
     for m in expand(after):
         high, rest = split(m)
         parts.append(dot(high, before_h) + dot(rest, before_h) + dot(high, before_l))
-    out_ref[...] = jnp.where(low, parts[0], parts[1])
+    return jnp.where(low, parts[0], parts[1])
+
+
+def product_kernel(upper_ref, own_ref, other_ref, out_ref):
+    out_ref[...] = multiply(upper_ref, own_ref, other_ref)
 
 
 def product(upper, own, other):
@@ -314,23 +327,33 @@
     return lines
 
 
-def chain_kernel(
-    res, ends_ref, edge_ref, coupling_ref, lower_ref, dinv_ref, spike_hbm, g_ref, out_ref, sol, spike_v, sems
+def product_and_edges_kernel(
+    upper_ref, own_ref, other_ref, ends_ref, edge_ref, coupling_ref, out_ref, terms_ref
 ):
-    n = g_ref.shape[0]
+    out_ref[...] = multiply(upper_ref, own_ref, other_ref)
+    code, edge = ends_ref[...], edge_ref[...]
+    for t in range(2):
+        terms_ref[t] = edge_terms(t, code, edge, lambda p: coupling_ref[t, LANES * p : LANES * (p + 1), :])
+
+
+def product_and_edges(upper, own, other, ends, edge, coupling):
+    return pl.pallas_call(
+        product_and_edges_kernel,
+        in_specs=[SMEM] + [VMEM] * 5,
+        out_specs=[VMEM] * 2,
+        out_shape=[
+            jax.ShapeDtypeStruct((LANES, LANES), F32),
+            jax.ShapeDtypeStruct((2, 8, LANES), F32),
+        ],
+        compiler_params=pltpu.CompilerParams(vmem_limit_bytes=4 << 20),
+        name="product_and_edges",
+    )(upper, own, other, ends, edge, coupling)
+
+
+def chain_kernel(res, terms_ref, lower_ref, dinv_ref, sol):
+    n = lower_ref.shape[0]
     blocks = n // SPAN
     ends = (0, n - 1)
-    spike_copies = [
-        pltpu.make_async_copy(spike_hbm.at[SPAN * b + SPAN - 1], spike_v.at[b], sems.at[b])
-        for b in range(1, blocks)
-    ]
-    for c in spike_copies:
-        c.start()
-    code, edge = ends_ref[...], edge_ref[...]
-    terms = [
-        edge_terms(t, code, edge, lambda p, t=t: coupling_ref[t, LANES * p : LANES * (p + 1), :])
-        for t in range(2)
-    ]
     sums, own = reduce_lanes(), own_lane()
     g = [None] * blocks
     for k in range(SPAN):
@@ -338,53 +361,44 @@
             e = SPAN * b + k
             balance = res[8 * e : 8 * e + 8, :]
             if e in ends:
-                balance = balance - terms[ends.index(e)]
+                balance = balance - terms_ref[ends.index(e)]
             if k > 0:
                 balance = balance - lying_matvec(g[b], lower_ref[e], sums, own)
             g[b] = lying_matvec(balance, dinv_ref[e], sums, own)
             sol[8 * e : 8 * e + 8, :] = g[b]
-    for c in spike_copies:
-        c.wait()
-    out = g[0]
-    for b in range(1, blocks):
-        out = lying_matvec(out, spike_v[b], sums, own) + g[b]
-    out_ref[...] = out
-    lane = iota((n, LANES), 1)
-    for p in range(2):
-        g_ref[:, LANES * p : LANES * (p + 1)] = jnp.where(
-            lane < WIDTH, sol[pl.ds(2 * p, n, stride=8), :], sol[pl.ds(2 * p + 1, n, stride=8), :]
-        )
-
-
-def chain(res, ends, edge, coupling, lower, dinv, spike):
+
+
+def chain(res, terms, lower, dinv):
     n = lower.shape[0]
-    blocks = n // SPAN
     return pl.pallas_call(
         chain_kernel,
-        in_specs=[VMEM] * 6 + [HBM],
-        out_specs=[VMEM, VMEM],
-        out_shape=[
-            jax.ShapeDtypeStruct((n, 256), F32),
-            jax.ShapeDtypeStruct((8, LANES), F32),
-        ],
-        scratch_shapes=[
-            pltpu.VMEM((8 * n, LANES), F32),
-            pltpu.VMEM((blocks, LANES, LANES), BF16),
-            pltpu.SemaphoreType.DMA((blocks,)),
-        ],
+        in_specs=[VMEM] * 4,
+        out_specs=VMEM,
+        out_shape=jax.ShapeDtypeStruct((8 * n, LANES), F32),
         compiler_params=pltpu.CompilerParams(vmem_limit_bytes=MOST),
         cost_estimate=pl.CostEstimate(flops=10**9, bytes_accessed=4 << 20, transcendentals=0),
         name="chain",
-    )(res, ends, edge, coupling, lower, dinv, spike)
-
-
-def outflow_kernel(me_ref, out_ref, t1_ref, t2_ref, t4_ref, send_ref):
+    )(res, terms, lower, dinv)
+
+
+def outflow_kernel(me_ref, sol, after_ref, t1_ref, t2_ref, t4_ref, g_ref, send_ref):
     me = me_ref[0]
-    out = out_ref[...]
+    n = g_ref.shape[0]
+    blocks = n // SPAN
+    lane = iota((n, LANES), 1)
     for p in range(2):
         lanes = slice(LANES * p, LANES * (p + 1))
-        w = jnp.where(iota((1, LANES), 1) < WIDTH, out[2 * p : 2 * p + 1], out[2 * p + 1 : 2 * p + 2])
-        w = jnp.broadcast_to(w, (8, LANES))
+        g = jnp.where(
+            lane < WIDTH, sol[pl.ds(2 * p, n, stride=8), :], sol[pl.ds(2 * p + 1, n, stride=8), :]
+        )
+        g_ref[:, lanes] = g
+        w = None
+        for b in range(blocks - 1, -1, -1):
+            e = SPAN * b + SPAN - 1
+            last = jnp.broadcast_to(g[e : e + 1], (8, LANES))
+            if b < blocks - 1:
+                last = times_map(last, split(expand(after_ref[b])[p]))
+            w = last if w is None else w + last
         levels = [w]
         for m, t_ref in ((1, t1_ref), (2, t2_ref), (4, t4_ref)):
             moved = times_map(w, split(expand(t_ref[...])[p]))
@@ -399,15 +413,19 @@
             send_ref[8 * half : 8 * half + 8, lanes] = message
 
 
-def outflow(me, out, t1, t2, t4):
+def outflow(me, sol, after, t1, t2, t4):
+    n = sol.shape[0] // 8
     return pl.pallas_call(
         outflow_kernel,
-        in_specs=[SMEM] + [VMEM] * 4,
-        out_specs=VMEM,
-        out_shape=jax.ShapeDtypeStruct((16, 256), F32),
+        in_specs=[SMEM] + [VMEM] * 5,
+        out_specs=[VMEM] * 2,
+        out_shape=[
+            jax.ShapeDtypeStruct((n, 256), F32),
+            jax.ShapeDtypeStruct((16, 256), F32),
+        ],
         compiler_params=pltpu.CompilerParams(vmem_limit_bytes=4 << 20),
         name="outflow",
-    )(me, out, t1, t2, t4)
+    )(me, sol, after, t1, t2, t4)
 
 
 def finish_kernel(me_ref, got_ref, g_ref, t1_ref, t2_ref, t4_ref, spike_ref, out_ref, raw):
@@ -513,13 +531,13 @@
     last = jnp.concatenate([low[n - 1 :], high[n - 1 :]], axis=0)
     to_mate, to_beyond = jnp.where(even, last, first), jnp.where(even, first, last)
     spike_x = as_it_lies(spike)
-    own1 = device_map(spike_x)
+    own1, after = device_map(spike_x)
     t1 = flip(own1, "stream", 1)
     beyond = between(to_beyond, "stream")
     mate = flip(to_mate, "stream", 1)
-    mate, own1, t1 = lax.optimization_barrier((mate, own1, t1))
+    own2 = product(me % 2, own1, t1)
+    mate, own2 = lax.optimization_barrier((mate, own2))
     edge = jnp.concatenate([jnp.where(even, beyond, mate), jnp.where(even, mate, beyond)], axis=0)
-    own2 = product(me % 2, own1, t1)
     t2 = flip(own2, "stream", 2)
     low, own2 = lax.optimization_barrier((low, own2))
 
@@ -533,10 +551,10 @@
         code, low, high, rhs, coupling_x, as_it_lies(lower), as_it_lies(dinv)
     )
     res, own2, t2 = lax.optimization_barrier((res, own2, t2))
-    own4 = product((me // 2) % 2, own2, t2)
+    own4, terms = product_and_edges((me // 2) % 2, own2, t2, ends, edge, ends_coupling)
     t4 = flip(own4, "stream", 4)
-    g, out = chain(res, ends, edge, ends_coupling, lower_v, dinv_v, spike_x)
-    send = outflow(me, out, t1, t2, t4)
+    sol = chain(res, terms, lower_v, dinv_v)
+    g, send = outflow(me, sol, after, t1, t2, t4)
     got = lax.all_to_all(send, "stream", 0, 0, tiled=True)
     return finish(me, got, g, t1, t2, t4, spike_x)
 

time: 47 us -> 45.9 us (0.977)
  starting transfers between devices: 18 us -> 17.3 us
    ppermute x5, starting transfers between devices: 10.4 us -> 8.83 us  [flip(): return lax.ppermute(x, axis, [(i, i ^ bit) for i in range(count)])]
    ppermute x2, starting transfers between devices: 7.51 us -> 8.49 us  [between(): return lax.ppermute(x, axis, pairs + [(j, i) for i, j in pairs])]
    pallas_call x3 -> x4, Pallas kernels: 9.5 us -> 9.39 us  [the longest x1 5.08 us: chain(): pl.pallas_call(chain_kernel, in_specs=[VMEM] * 4, out_specs=VMEM, out_sha...]
  transfers between devices with their start and end apart: 7 -> 7, of which waited for: 0 -> 0; matrix products, arithmetic and copies ran while one was open for 0% -> 0% of each run, Pallas kernels for 28% -> 27%
where the time goes in v3:
time: 45.9 us; the launch traced here: 45.7 us
  starting transfers between devices  17.3 us (38%)
  Pallas kernels  16.2 us (35%)
  blocking collectives  11.8 us (26%)
    all_to_all x1, blocking collectives, on_device(): got = lax.all_to_all(send, 'stream', 0, 0, tiled=True)  11.8 us
    ppermute x5, starting transfers between devices, flip(): return lax.ppermute(x, axis, [(i, i ^ bit) for i in range(count)])  8.83 us
    ppermute x2, starting transfers between devices, between(): return lax.ppermute(x, axis, pairs + [(j, i) for i, j in pairs])  8.49 us
    pallas_call x1, Pallas kernels, chain(): pl.pallas_call(chain_kernel, in_specs=[VMEM] * 4, out_specs=VMEM, out_sha...  5.08 us
    pallas_call x1, Pallas kernels, residual(): pl.pallas_call(residual_kernel, in_specs=[VMEM] * 4 + [HBM] * 3, out_spec...  4.21 us
    pallas_call x1, Pallas kernels, device_map(): pl.pallas_call(device_map_kernel, in_specs=[HBM], out_specs=[VMEM] * 2, o...  2.74 us
    pallas_call x1, Pallas kernels, finish(): pl.pallas_call(finish_kernel, in_specs=[pl.BlockSpec(memory_space=pltpu.S...  2.35 us
    pallas_call x1, Pallas kernels, outflow(): pl.pallas_call(outflow_kernel, in_specs=[SMEM] + [VMEM] * 5, out_specs=[V...  1.11 us
  transfers between devices with their start and end apart: 7, of which 0 were waited for; matrix products, arithmetic and copies ran while one was open for 0% of the time, Pallas kernels for 27%

profile of v3, /device:TPU:7, one launch (start us, length us, event | category | flops | bytes accessed | tf_op | source)
XLA Modules:
  0.0 45.7 jit_solution(8714371382798143218)
XLA Ops:
  0.0 5.0 %collective-permute-start = (f32[64,256]{1,0:T(8,128)}, f32[64,256]{1,0:T(8,128)S(1)}, u32[]{:S(2)}, u32[]{:S(2)}) collective-permute-start(f32[64,256]{1,0:T(8,128)} %param.9), channel_id=1, source_target_pairs={{1,2},{3,4},{5,6},{7,8},{9,10},{11,12},{13,14},{2,1},{4,3},{6,5},{... | collective-permute-start | bytes 196616 | tf_op jit(solution)/shard_map/ppermute | solution.py:514
  5.1 0.1 collective-permute-start.1
  5.2 2.7 %device_map.1 = (f32[128,128]{1,0:T(8,128)S(1)}, f32[3,128,128]{2,1,0:T(8,128)S(1)}) custom-call(bf16[64,128,128]{2,1,0:T(8,128)(2,1)} %bitcast.28), custom_call_target="tpu_custom_call" | custom-call | tf_op jit(solution)/shard_map/device_map/pallas_call | solution.py:113
  7.9 1.0 %collective-permute-start.3 = (f32[128,128]{1,0:T(8,128)S(1)}, f32[128,128]{1,0:T(8,128)S(1)}, u32[]{:S(2)}, u32[]{:S(2)}) collective-permute-start(f32[128,128]{1,0:T(8,128)S(1)} %get-tuple-element.23.own_ref), channel_id=1, source_target_pairs={{0,16},{16,0},{32,48},{48,32},{64,80},{80,64},{96,112},{112,96},{1... | collective-permute-start | bytes 196616 | tf_op jit(solution)/shard_map/ppermute | solution.py:508
  9.0 0.0 collective-permute-done
  9.0 0.0 collective-permute-done.1
  9.0 1.7 %collective-permute-start.2 = (f32[2,256]{1,0:T(2,128)S(1)}, f32[2,256]{1,0:T(2,128)S(1)}, u32[]{:S(2)}, u32[]{:S(2)}) collective-permute-start(f32[2,256]{1,0:T(2,128)S(1)} %get-tuple-element.50), channel_id=1, source_target_pairs={{0,16},{16,0},{32,48},{48,32},{64,80},{80,64},{96,112},{112,96},{1... | collective-permute-start | bytes 6152 | tf_op jit(solution)/shard_map/ppermute | solution.py:508
  10.7 0.0 copy-done.3
  10.7 0.1 fusion.1
  10.8 3.4 %collective-permute-start.5 = (f32[2,256]{1,0:T(2,128)S(1)}, f32[2,256]{1,0:T(2,128)S(1)}, u32[]{:S(2)}, u32[]{:S(2)}) collective-permute-start(f32[2,256]{1,0:T(2,128)S(1)} %get-tuple-element.49), channel_id=1, source_target_pairs={{16,32},{48,64},{80,96},{112,128},{144,160},{176,192},{208,224},{3... | collective-permute-start | bytes 6152 | tf_op jit(solution)/shard_map/ppermute | solution.py:514
  14.2 0.0 collective-permute-done.3.other_ref.t1_ref
  14.3 0.3 product.1.own_ref
  14.5 0.0 collective-permute-done.2
  14.5 1.7 %collective-permute-start.4 = (f32[128,128]{1,0:T(8,128)S(1)}, f32[128,128]{1,0:T(8,128)S(1)}, u32[]{:S(2)}, u32[]{:S(2)}) collective-permute-start(f32[128,128]{1,0:T(8,128)S(1)} %product.1.own_ref), channel_id=1, source_target_pairs={{0,32},{16,48},{32,0},{48,16},{64,96},{80,112},{96,64},{112,80},{1... | collective-permute-start | bytes 196616 | tf_op jit(solution)/shard_map/ppermute | solution.py:508
  16.3 4.2 %residual.1 = (f32[512,128]{1,0:T(8,128)S(1)}, f32[2,512]{1,0:T(2,128)S(1)}, bf16[2,256,128]{2,1,0:T(8,128)(2,1)S(1)}, bf16[64,128,128]{2,1,0:T(8,128)(2,1)S(1)}, bf16[64,128,128]{2,1,0:T(8,128)(2,1)S(1)}) custom-call(f32[8,64]{1,0:T(8,128)S(1)} %bitcast.31, f32[64,256]{1,0:T(8,128)S(1)} %get-tuple-element.25.low_ref, ...), custom_call_target="tpu_custom_call" | custom-call | flops 100000000 | bytes 4194304 | tf_op jit(solution)/shard_map/residual/pallas_call | solution.py:285
  20.5 0.0 collective-permute-done.5
  20.5 0.0 collective-permute-done.4.other_ref.t2_ref
  20.5 0.5 %product_and_edges.1 = (f32[128,128]{1,0:T(8,128)S(1)}, f32[2,8,128]{2,1,0:T(8,128)S(1)}) custom-call(s32[1]{0:T(128)S(6)} %select_n.74.upper_ref, f32[128,128]{1,0:T(8,128)S(1)} %product.1.own_ref, f32[128,128]{1,0:T(8,128)S(1)} %collective-permute-done.4.other_ref.t2_ref, f32[2,512]{1,0:T(2,128)S(1)} %get-tuple-element.31.ends_ref, ...), custom_call_target="tpu_custom_call" | custom-call | tf_op jit(solution)/shard_map/product_and_edges/pallas_call | solution.py:340
  21.0 4.3 %collective-permute-start.6 = (f32[128,128]{1,0:T(8,128)S(1)}, f32[128,128]{1,0:T(8,128)S(1)}, u32[]{:S(2)}, u32[]{:S(2)}) collective-permute-start(f32[128,128]{1,0:T(8,128)S(1)} %get-tuple-element.38), channel_id=1, source_target_pairs={{0,64},{16,80},{32,96},{48,112},{64,0},{80,16},{96,32},{112,48},{1... | collective-permute-start | bytes 196616 | tf_op jit(solution)/shard_map/ppermute | solution.py:508
  25.3 5.1 %chain.1.sol = f32[512,128]{1,0:T(8,128)S(1)} custom-call(f32[512,128]{1,0:T(8,128)S(1)} %get-tuple-element.28.res, f32[2,8,128]{2,1,0:T(8,128)S(1)} %get-tuple-element.34.terms_ref, bf16[64,128,128]{2,1,0:T(8,128)(2,1)S(1)} %get-tuple-element.35.lower_ref, bf16[64,128,128]{2,1,0:T(8,128)(2,1)S(1)} %get-tuple-element.36.dinv_ref), custom_call_target="tpu_custom_call" | custom-call | flops 1000000000 | bytes 4194304 | tf_op jit(solution)/shard_map/chain/pallas_call | solution.py:373
  30.3 0.0 collective-permute-done.6.t4_ref
  30.4 1.1 %outflow.1 = (f32[64,256]{1,0:T(8,128)S(1)}, f32[16,256]{1,0:T(8,128)S(1)}) custom-call(s32[1]{0:T(128)} %bitcast.me_ref, f32[512,128]{1,0:T(8,128)S(1)} %chain.1.sol, f32[3,128,128]{2,1,0:T(8,128)S(1)} %get-tuple-element.37.after_ref, f32[128,128]{1,0:T(8,128)S(1)} %collective-permute-done.3.other_ref.t1_ref, ...), custom_call_target="tpu_custom_call" | custom-call | tf_op jit(solution)/shard_map/outflow/pallas_call | solution.py:418
  31.5 11.8 %all_to_all.11 = f32[16,1,256]{2,1,0:T(1,128)S(1)} all-to-all(f32[16,1,256]{2,1,0:T(1,128)S(1)} %copy.17), channel_id=1, replica_groups=mesh['stream'=16,'cross'=16] {'stream'}, dimensions={0} | all-to-all | bytes 32768 | tf_op jit(solution)/shard_map/all_to_all | solution.py:558
  43.3 2.3 %finish.1 = f32[64,256]{1,0:T(8,128)} custom-call(s32[1]{0:T(128)} %bitcast.me_ref, f32[16,256]{1,0:T(8,128)S(1)} %bitcast.30, f32[64,256]{1,0:T(8,128)S(1)} %get-tuple-element.40.g_ref, f32[128,128]{1,0:T(8,128)S(1)} %collective-permute-done.3.other_ref.t1_ref, f32[128,128]{1,0:T(8,128)S(1)} %collective-permute-done.4.other_ref.t2_ref, ...), custom_call_target="tpu_custom_call" | custom-call | tf_op jit(solution)/shard_map/finish/pallas_call | solution.py:495
  (15 shorter events, 0.1 us)
Async XLA Ops:
  0.0 10.7 %copy-start.3 = (s32[64,4,2]{0,2,1:T(2,128)S(1)}, s32[64,4,2]{0,2,1:T(2,128)}, u32[]{:S(2)}) copy-start(s32[64,4,2]{0,2,1:T(2,128)} %param.14) | copy-start | bytes 6148
  0.0 10.7 %copy-start.2 = (s32[64,4,2]{0,2,1:T(2,128)S(1)}, s32[64,4,2]{0,2,1:T(2,128)}, u32[]{:S(2)}) copy-start(s32[64,4,2]{0,2,1:T(2,128)} %param.15) | copy-start | bytes 6148
  0.0 16.3 %copy-start.1 = (f32[64,256]{1,0:T(8,128)S(1)}, f32[64,256]{1,0:T(8,128)}, u32[]{:S(2)}) copy-start(f32[64,256]{1,0:T(8,128)} %rhs_ref.1) | copy-start | bytes 196612
  0.0 8.9 %collective-permute-start = (f32[64,256]{1,0:T(8,128)}, f32[64,256]{1,0:T(8,128)S(1)}, u32[]{:S(2)}, u32[]{:S(2)}) collective-permute-start(f32[64,256]{1,0:T(8,128)} %param.9), channel_id=1, source_target_pairs={{1,2},{3,4},{5,6},{7,8},{9,10},{11,12},{13,14},{2,1},{4,3},{6,5},{... | collective-permute-start | bytes 196616 | tf_op jit(solution)/shard_map/ppermute | solution.py:514
  5.1 3.9 %collective-permute-start.1 = (f32[64,256]{1,0:T(8,128)}, f32[64,256]{1,0:T(8,128)S(1)}, u32[]{:S(2)}, u32[]{:S(2)}) collective-permute-start(f32[64,256]{1,0:T(8,128)} %param.9), channel_id=1, source_target_pairs={{0,1},{1,0},{2,3},{3,2},{4,5},{5,4},{6,7},{7,6},{8,9},{9,8},{10,11... | collective-permute-start | bytes 196616 | tf_op jit(solution)/shard_map/ppermute | solution.py:508
  7.9 6.3 %collective-permute-start.3 = (f32[128,128]{1,0:T(8,128)S(1)}, f32[128,128]{1,0:T(8,128)S(1)}, u32[]{:S(2)}, u32[]{:S(2)}) collective-permute-start(f32[128,128]{1,0:T(8,128)S(1)} %get-tuple-element.23.own_ref), channel_id=1, source_target_pairs={{0,16},{16,0},{32,48},{48,32},{64,80},{80,64},{96,112},{112,96},{1... | collective-permute-start | bytes 196616 | tf_op jit(solution)/shard_map/ppermute | solution.py:508
  9.0 5.5 %collective-permute-start.2 = (f32[2,256]{1,0:T(2,128)S(1)}, f32[2,256]{1,0:T(2,128)S(1)}, u32[]{:S(2)}, u32[]{:S(2)}) collective-permute-start(f32[2,256]{1,0:T(2,128)S(1)} %get-tuple-element.50), channel_id=1, source_target_pairs={{0,16},{16,0},{32,48},{48,32},{64,80},{80,64},{96,112},{112,96},{1... | collective-permute-start | bytes 6152 | tf_op jit(solution)/shard_map/ppermute | solution.py:508
  10.8 9.7 %collective-permute-start.5 = (f32[2,256]{1,0:T(2,128)S(1)}, f32[2,256]{1,0:T(2,128)S(1)}, u32[]{:S(2)}, u32[]{:S(2)}) collective-permute-start(f32[2,256]{1,0:T(2,128)S(1)} %get-tuple-element.49), channel_id=1, source_target_pairs={{16,32},{48,64},{80,96},{112,128},{144,160},{176,192},{208,224},{3... | collective-permute-start | bytes 6152 | tf_op jit(solution)/shard_map/ppermute | solution.py:514
  14.5 6.0 %collective-permute-start.4 = (f32[128,128]{1,0:T(8,128)S(1)}, f32[128,128]{1,0:T(8,128)S(1)}, u32[]{:S(2)}, u32[]{:S(2)}) collective-permute-start(f32[128,128]{1,0:T(8,128)S(1)} %product.1.own_ref), channel_id=1, source_target_pairs={{0,32},{16,48},{32,0},{48,16},{64,96},{80,112},{96,64},{112,80},{1... | collective-permute-start | bytes 196616 | tf_op jit(solution)/shard_map/ppermute | solution.py:508
  21.0 9.4 %collective-permute-start.6 = (f32[128,128]{1,0:T(8,128)S(1)}, f32[128,128]{1,0:T(8,128)S(1)}, u32[]{:S(2)}, u32[]{:S(2)}) collective-permute-start(f32[128,128]{1,0:T(8,128)S(1)} %get-tuple-element.38), channel_id=1, source_target_pairs={{0,64},{16,80},{32,96},{48,112},{64,0},{80,16},{96,32},{112,48},{1... | collective-permute-start | bytes 196616 | tf_op jit(solution)/shard_map/ppermute | solution.py:508
  25.3 18.1 %copy-start = (bf16[64,4,4096]{2,1,0:T(4,128)(2,1)S(1)}, bf16[64,4,4096]{2,1,0:T(4,128)(2,1)}, u32[]{:S(2)}) copy-start(bf16[64,4,4096]{2,1,0:T(4,128)(2,1)} %param.12) | copy-start | bytes 6291460

commit v4 on v3

--- a/solution.py
+++ b/solution.py
@@ -526,7 +526,7 @@
     near = flip(previous, "cross", 1)
     low = jnp.where(cross % 2 == 0, far, near)
     high = jnp.where(cross % 2 == 0, near, far)
-    even = stream % 2 == 0
+    even, odd = stream % 2 == 0, stream % 2 == 1
     first = jnp.concatenate([low[:1], high[:1]], axis=0)
     last = jnp.concatenate([low[n - 1 :], high[n - 1 :]], axis=0)
     to_mate, to_beyond = jnp.where(even, last, first), jnp.where(even, first, last)
@@ -537,7 +537,7 @@
     mate = flip(to_mate, "stream", 1)
     own2 = product(me % 2, own1, t1)
     mate, own2 = lax.optimization_barrier((mate, own2))
-    edge = jnp.concatenate([jnp.where(even, beyond, mate), jnp.where(even, mate, beyond)], axis=0)
+    edge = jnp.concatenate([jnp.where(odd, mate, beyond), jnp.where(odd, beyond, mate)], axis=0)
     t2 = flip(own2, "stream", 2)
     low, own2 = lax.optimization_barrier((low, own2))
 

time: 45.9 us -> 45.9 us (level)
  no operation moved by 1% of the time
where the time goes in v4:
time: 45.9 us; the launch traced here: 45.7 us
  starting transfers between devices  17.3 us (38%)
  Pallas kernels  16.2 us (35%)
  blocking collectives  11.8 us (26%)
    all_to_all x1, blocking collectives, on_device(): got = lax.all_to_all(send, 'stream', 0, 0, tiled=True)  11.8 us
    ppermute x5, starting transfers between devices, flip(): return lax.ppermute(x, axis, [(i, i ^ bit) for i in range(count)])  8.83 us
    ppermute x2, starting transfers between devices, between(): return lax.ppermute(x, axis, pairs + [(j, i) for i, j in pairs])  8.49 us
    pallas_call x1, Pallas kernels, chain(): pl.pallas_call(chain_kernel, in_specs=[VMEM] * 4, out_specs=VMEM, out_sha...  5.08 us
    pallas_call x1, Pallas kernels, residual(): pl.pallas_call(residual_kernel, in_specs=[VMEM] * 4 + [HBM] * 3, out_spec...  4.21 us
    pallas_call x1, Pallas kernels, device_map(): pl.pallas_call(device_map_kernel, in_specs=[HBM], out_specs=[VMEM] * 2, o...  2.74 us
    pallas_call x1, Pallas kernels, finish(): pl.pallas_call(finish_kernel, in_specs=[pl.BlockSpec(memory_space=pltpu.S...  2.35 us
    pallas_call x1, Pallas kernels, outflow(): pl.pallas_call(outflow_kernel, in_specs=[SMEM] + [VMEM] * 5, out_specs=[V...  1.11 us
  transfers between devices with their start and end apart: 7, of which 0 were waited for; matrix products, arithmetic and copies ran while one was open for 0% of the time, Pallas kernels for 27%

profile of v4, /device:TPU:7, one launch (start us, length us, event | category | flops | bytes accessed | tf_op | source)
XLA Modules:
  0.0 45.7 jit_solution(3111502433078401641)
XLA Ops:
  0.0 5.0 %collective-permute-start = (f32[64,256]{1,0:T(8,128)}, f32[64,256]{1,0:T(8,128)S(1)}, u32[]{:S(2)}, u32[]{:S(2)}) collective-permute-start(f32[64,256]{1,0:T(8,128)} %param.9), channel_id=1, source_target_pairs={{1,2},{3,4},{5,6},{7,8},{9,10},{11,12},{13,14},{2,1},{4,3},{6,5},{... | collective-permute-start | bytes 196616 | tf_op jit(solution)/shard_map/ppermute | solution.py:514
  5.1 0.1 collective-permute-start.1
  5.2 2.7 %device_map.1 = (f32[128,128]{1,0:T(8,128)S(1)}, f32[3,128,128]{2,1,0:T(8,128)S(1)}) custom-call(bf16[64,128,128]{2,1,0:T(8,128)(2,1)} %bitcast.28), custom_call_target="tpu_custom_call" | custom-call | tf_op jit(solution)/shard_map/device_map/pallas_call | solution.py:113
  7.9 1.0 %collective-permute-start.3 = (f32[128,128]{1,0:T(8,128)S(1)}, f32[128,128]{1,0:T(8,128)S(1)}, u32[]{:S(2)}, u32[]{:S(2)}) collective-permute-start(f32[128,128]{1,0:T(8,128)S(1)} %get-tuple-element.23.own_ref), channel_id=1, source_target_pairs={{0,16},{16,0},{32,48},{48,32},{64,80},{80,64},{96,112},{112,96},{1... | collective-permute-start | bytes 196616 | tf_op jit(solution)/shard_map/ppermute | solution.py:508
  9.0 0.0 collective-permute-done
  9.0 0.0 collective-permute-done.1
  9.0 1.7 %collective-permute-start.2 = (f32[2,256]{1,0:T(2,128)S(1)}, f32[2,256]{1,0:T(2,128)S(1)}, u32[]{:S(2)}, u32[]{:S(2)}) collective-permute-start(f32[2,256]{1,0:T(2,128)S(1)} %get-tuple-element.50), channel_id=1, source_target_pairs={{0,16},{16,0},{32,48},{48,32},{64,80},{80,64},{96,112},{112,96},{1... | collective-permute-start | bytes 6152 | tf_op jit(solution)/shard_map/ppermute | solution.py:508
  10.7 0.0 copy-done.3
  10.7 0.1 fusion.1
  10.8 3.4 %collective-permute-start.5 = (f32[2,256]{1,0:T(2,128)S(1)}, f32[2,256]{1,0:T(2,128)S(1)}, u32[]{:S(2)}, u32[]{:S(2)}) collective-permute-start(f32[2,256]{1,0:T(2,128)S(1)} %get-tuple-element.49), channel_id=1, source_target_pairs={{16,32},{48,64},{80,96},{112,128},{144,160},{176,192},{208,224},{3... | collective-permute-start | bytes 6152 | tf_op jit(solution)/shard_map/ppermute | solution.py:514
  14.2 0.0 collective-permute-done.3.other_ref.t1_ref
  14.3 0.3 product.1.own_ref
  14.5 0.0 collective-permute-done.2
  14.5 1.7 %collective-permute-start.4 = (f32[128,128]{1,0:T(8,128)S(1)}, f32[128,128]{1,0:T(8,128)S(1)}, u32[]{:S(2)}, u32[]{:S(2)}) collective-permute-start(f32[128,128]{1,0:T(8,128)S(1)} %product.1.own_ref), channel_id=1, source_target_pairs={{0,32},{16,48},{32,0},{48,16},{64,96},{80,112},{96,64},{112,80},{1... | collective-permute-start | bytes 196616 | tf_op jit(solution)/shard_map/ppermute | solution.py:508
  16.3 4.2 %residual.1 = (f32[512,128]{1,0:T(8,128)S(1)}, f32[2,512]{1,0:T(2,128)S(1)}, bf16[2,256,128]{2,1,0:T(8,128)(2,1)S(1)}, bf16[64,128,128]{2,1,0:T(8,128)(2,1)S(1)}, bf16[64,128,128]{2,1,0:T(8,128)(2,1)S(1)}) custom-call(f32[8,64]{1,0:T(8,128)S(1)} %bitcast.31, f32[64,256]{1,0:T(8,128)S(1)} %get-tuple-element.25.low_ref, ...), custom_call_target="tpu_custom_call" | custom-call | flops 100000000 | bytes 4194304 | tf_op jit(solution)/shard_map/residual/pallas_call | solution.py:285
  20.5 0.0 collective-permute-done.5
  20.5 0.0 collective-permute-done.4.other_ref.t2_ref
  20.5 0.5 %product_and_edges.1 = (f32[128,128]{1,0:T(8,128)S(1)}, f32[2,8,128]{2,1,0:T(8,128)S(1)}) custom-call(s32[1]{0:T(128)S(6)} %select_n.78.upper_ref, f32[128,128]{1,0:T(8,128)S(1)} %product.1.own_ref, f32[128,128]{1,0:T(8,128)S(1)} %collective-permute-done.4.other_ref.t2_ref, f32[2,512]{1,0:T(2,128)S(1)} %get-tuple-element.31.ends_ref, ...), custom_call_target="tpu_custom_call" | custom-call | tf_op jit(solution)/shard_map/product_and_edges/pallas_call | solution.py:340
  21.0 4.3 %collective-permute-start.6 = (f32[128,128]{1,0:T(8,128)S(1)}, f32[128,128]{1,0:T(8,128)S(1)}, u32[]{:S(2)}, u32[]{:S(2)}) collective-permute-start(f32[128,128]{1,0:T(8,128)S(1)} %get-tuple-element.38), channel_id=1, source_target_pairs={{0,64},{16,80},{32,96},{48,112},{64,0},{80,16},{96,32},{112,48},{1... | collective-permute-start | bytes 196616 | tf_op jit(solution)/shard_map/ppermute | solution.py:508
  25.3 5.1 %chain.1.sol = f32[512,128]{1,0:T(8,128)S(1)} custom-call(f32[512,128]{1,0:T(8,128)S(1)} %get-tuple-element.28.res, f32[2,8,128]{2,1,0:T(8,128)S(1)} %get-tuple-element.34.terms_ref, bf16[64,128,128]{2,1,0:T(8,128)(2,1)S(1)} %get-tuple-element.35.lower_ref, bf16[64,128,128]{2,1,0:T(8,128)(2,1)S(1)} %get-tuple-element.36.dinv_ref), custom_call_target="tpu_custom_call" | custom-call | flops 1000000000 | bytes 4194304 | tf_op jit(solution)/shard_map/chain/pallas_call | solution.py:373
  30.3 0.0 collective-permute-done.6.t4_ref
  30.4 1.1 %outflow.1 = (f32[64,256]{1,0:T(8,128)S(1)}, f32[16,256]{1,0:T(8,128)S(1)}) custom-call(s32[1]{0:T(128)} %bitcast.me_ref, f32[512,128]{1,0:T(8,128)S(1)} %chain.1.sol, f32[3,128,128]{2,1,0:T(8,128)S(1)} %get-tuple-element.37.after_ref, f32[128,128]{1,0:T(8,128)S(1)} %collective-permute-done.3.other_ref.t1_ref, ...), custom_call_target="tpu_custom_call" | custom-call | tf_op jit(solution)/shard_map/outflow/pallas_call | solution.py:418
  31.5 11.8 %all_to_all.11 = f32[16,1,256]{2,1,0:T(1,128)S(1)} all-to-all(f32[16,1,256]{2,1,0:T(1,128)S(1)} %copy.17), channel_id=1, replica_groups=mesh['stream'=16,'cross'=16] {'stream'}, dimensions={0} | all-to-all | bytes 32768 | tf_op jit(solution)/shard_map/all_to_all | solution.py:558
  43.3 2.3 %finish.1 = f32[64,256]{1,0:T(8,128)} custom-call(s32[1]{0:T(128)} %bitcast.me_ref, f32[16,256]{1,0:T(8,128)S(1)} %bitcast.30, f32[64,256]{1,0:T(8,128)S(1)} %get-tuple-element.40.g_ref, f32[128,128]{1,0:T(8,128)S(1)} %collective-permute-done.3.other_ref.t1_ref, f32[128,128]{1,0:T(8,128)S(1)} %collective-permute-done.4.other_ref.t2_ref, ...), custom_call_target="tpu_custom_call" | custom-call | tf_op jit(solution)/shard_map/finish/pallas_call | solution.py:495
  (15 shorter events, 0.1 us)
Async XLA Ops:
  0.0 10.7 %copy-start.3 = (s32[64,4,2]{0,2,1:T(2,128)S(1)}, s32[64,4,2]{0,2,1:T(2,128)}, u32[]{:S(2)}) copy-start(s32[64,4,2]{0,2,1:T(2,128)} %param.14) | copy-start | bytes 6148
  0.0 10.7 %copy-start.2 = (s32[64,4,2]{0,2,1:T(2,128)S(1)}, s32[64,4,2]{0,2,1:T(2,128)}, u32[]{:S(2)}) copy-start(s32[64,4,2]{0,2,1:T(2,128)} %param.15) | copy-start | bytes 6148
  0.0 16.3 %copy-start.1 = (f32[64,256]{1,0:T(8,128)S(1)}, f32[64,256]{1,0:T(8,128)}, u32[]{:S(2)}) copy-start(f32[64,256]{1,0:T(8,128)} %rhs_ref.1) | copy-start | bytes 196612
  0.0 8.9 %collective-permute-start = (f32[64,256]{1,0:T(8,128)}, f32[64,256]{1,0:T(8,128)S(1)}, u32[]{:S(2)}, u32[]{:S(2)}) collective-permute-start(f32[64,256]{1,0:T(8,128)} %param.9), channel_id=1, source_target_pairs={{1,2},{3,4},{5,6},{7,8},{9,10},{11,12},{13,14},{2,1},{4,3},{6,5},{... | collective-permute-start | bytes 196616 | tf_op jit(solution)/shard_map/ppermute | solution.py:514
  5.1 3.9 %collective-permute-start.1 = (f32[64,256]{1,0:T(8,128)}, f32[64,256]{1,0:T(8,128)S(1)}, u32[]{:S(2)}, u32[]{:S(2)}) collective-permute-start(f32[64,256]{1,0:T(8,128)} %param.9), channel_id=1, source_target_pairs={{0,1},{1,0},{2,3},{3,2},{4,5},{5,4},{6,7},{7,6},{8,9},{9,8},{10,11... | collective-permute-start | bytes 196616 | tf_op jit(solution)/shard_map/ppermute | solution.py:508
  7.9 6.3 %collective-permute-start.3 = (f32[128,128]{1,0:T(8,128)S(1)}, f32[128,128]{1,0:T(8,128)S(1)}, u32[]{:S(2)}, u32[]{:S(2)}) collective-permute-start(f32[128,128]{1,0:T(8,128)S(1)} %get-tuple-element.23.own_ref), channel_id=1, source_target_pairs={{0,16},{16,0},{32,48},{48,32},{64,80},{80,64},{96,112},{112,96},{1... | collective-permute-start | bytes 196616 | tf_op jit(solution)/shard_map/ppermute | solution.py:508
  9.0 5.5 %collective-permute-start.2 = (f32[2,256]{1,0:T(2,128)S(1)}, f32[2,256]{1,0:T(2,128)S(1)}, u32[]{:S(2)}, u32[]{:S(2)}) collective-permute-start(f32[2,256]{1,0:T(2,128)S(1)} %get-tuple-element.50), channel_id=1, source_target_pairs={{0,16},{16,0},{32,48},{48,32},{64,80},{80,64},{96,112},{112,96},{1... | collective-permute-start | bytes 6152 | tf_op jit(solution)/shard_map/ppermute | solution.py:508
  10.8 9.7 %collective-permute-start.5 = (f32[2,256]{1,0:T(2,128)S(1)}, f32[2,256]{1,0:T(2,128)S(1)}, u32[]{:S(2)}, u32[]{:S(2)}) collective-permute-start(f32[2,256]{1,0:T(2,128)S(1)} %get-tuple-element.49), channel_id=1, source_target_pairs={{16,32},{48,64},{80,96},{112,128},{144,160},{176,192},{208,224},{3... | collective-permute-start | bytes 6152 | tf_op jit(solution)/shard_map/ppermute | solution.py:514
  14.5 6.0 %collective-permute-start.4 = (f32[128,128]{1,0:T(8,128)S(1)}, f32[128,128]{1,0:T(8,128)S(1)}, u32[]{:S(2)}, u32[]{:S(2)}) collective-permute-start(f32[128,128]{1,0:T(8,128)S(1)} %product.1.own_ref), channel_id=1, source_target_pairs={{0,32},{16,48},{32,0},{48,16},{64,96},{80,112},{96,64},{112,80},{1... | collective-permute-start | bytes 196616 | tf_op jit(solution)/shard_map/ppermute | solution.py:508
  21.0 9.4 %collective-permute-start.6 = (f32[128,128]{1,0:T(8,128)S(1)}, f32[128,128]{1,0:T(8,128)S(1)}, u32[]{:S(2)}, u32[]{:S(2)}) collective-permute-start(f32[128,128]{1,0:T(8,128)S(1)} %get-tuple-element.38), channel_id=1, source_target_pairs={{0,64},{16,80},{32,96},{48,112},{64,0},{80,16},{96,32},{112,48},{1... | collective-permute-start | bytes 196616 | tf_op jit(solution)/shard_map/ppermute | solution.py:508
  25.3 18.1 %copy-start = (bf16[64,4,4096]{2,1,0:T(4,128)(2,1)S(1)}, bf16[64,4,4096]{2,1,0:T(4,128)(2,1)}, u32[]{:S(2)}) copy-start(bf16[64,4,4096]{2,1,0:T(4,128)(2,1)} %param.12) | copy-start | bytes 6291460
